TPU v7x, 32 devices: a whole 2x2x4 slice. The times are simulated.
32 devices in a mesh: groups: 2 (over y), fil: 4 (over z), col: 4 (over x, core).
Axes of the slice: x: 2, y: 2, z: 4, core: 2. Of those that a mesh axis runs over, the one named last changes fastest.
Arguments:
- geometry: float32 [6, 6144], P(None, ('groups', 'fil', 'col')), parts along dimension 1, may hold values from -4 to 4, as said below
- net_ids: int32 [6144], P(('groups', 'fil', 'col')), parts along dimension 0, may hold values from 0 to 3
- layers: int32 [6144], P(('groups', 'fil', 'col')), parts along dimension 0, may hold values from 0 to 7
- trial_modes: bfloat16 [6144, 32], P(('groups', 'fil', 'col')), parts along dimension 0, may hold values from -6 to 6
- low_edge: float32 [2], P('groups'), parts along dimension 0, may hold values from 1 to 3
- high_edge: float32 [2], P('groups'), parts along dimension 0, may hold values from 40 to 80
Outputs:
- ritz_basis: float32 [6144, 32], P(('groups', 'fil', 'col')), parts along dimension 0
- projected: float32 [64, 32], P('groups'), parts along dimension 0
There are 2 independent parts, one for each index of `groups`. A program takes and returns all parts, laid end to end along the dimension named above; each array names one. Nothing has to cross between parts.
Inputs may be any that keep to these rules, and one draw needn't show every extreme that they name: `geometry`: rows 0 and 1 lie in [0, 1]; row 5 lies in [0.002, 0.006].
All inputs are finite; a program needn't handle non-finite values.
Results may differ from a plain program's by a relative error of at most 0.00055.
The roundings to bfloat16 on the way count: a program that leaves them out, or rounds other values in their place, can miss the bound.
Values may be sent and summed in bfloat16 or wider, within the bound.
No kernel may reach another device: no remote copies, remote signals or barrier semaphores. Data moves between devices by JAX's collectives and lax.ppermute only.
A program may use at most 64 MiB of HBM per device.

v0:
```python
import math

import jax
import jax.numpy as jnp
from jax import lax
from jax.sharding import PartitionSpec as P

SHIELD_FACTOR = 0.5
LAYER_PITCH = 0.02


def features(geometry, net_ids, layers):
    height = layers.astype(jnp.float32) * LAYER_PITCH
    return jnp.stack(
        [
            geometry[0],
            geometry[1],
            height,
            geometry[2],
            geometry[3],
            geometry[4],
            geometry[5],
            net_ids.astype(jnp.float32),
        ],
        axis=0,
    )


def kernel_tile(row_feat, col_feat, kernel_scale):
    delta_x = row_feat[0][:, None] - col_feat[0][None, :]
    delta_y = row_feat[1][:, None] - col_feat[1][None, :]
    delta_z = row_feat[2][:, None] - col_feat[2][None, :]
    radius_sq = (
        row_feat[6][:, None] * row_feat[6][:, None] + col_feat[6][None, :] * col_feat[6][None, :]
    )
    spread = delta_x * delta_x + delta_y * delta_y + delta_z * delta_z + radius_sq
    alignment = (
        row_feat[3][:, None] * col_feat[3][None, :]
        + row_feat[4][:, None] * col_feat[4][None, :]
        + row_feat[5][:, None] * col_feat[5][None, :]
    )
    couple = jnp.where(row_feat[7][:, None] == col_feat[7][None, :], 1.0, SHIELD_FACTOR)
    return (alignment * couple * lax.rsqrt(spread) * kernel_scale).astype(jnp.bfloat16)


def column_span(length, tile_rows, shard_rows):
    span_limit = max(shard_rows, (1 << 20) // tile_rows)
    span_cols = shard_rows
    while span_cols * 2 <= span_limit and length % (span_cols * 2) == 0:
        span_cols = span_cols * 2
    return span_cols


def accumulate(running, row_feat, part_feats, gathered, kernel_scale, span_cols):
    turns = gathered.shape[0] // span_cols

    def one_span(turn_index, partial_sum):
        offset = turn_index * span_cols
        span_feats = lax.dynamic_slice_in_dim(part_feats, offset, span_cols, 1)
        span_modes = lax.dynamic_slice_in_dim(gathered, offset, span_cols, 0)
        tile_vals = kernel_tile(row_feat, span_feats, kernel_scale)
        return partial_sum + jnp.dot(tile_vals, span_modes, preferred_element_type=jnp.float32)

    return lax.fori_loop(0, turns, one_span, running)


def shards(geometry, net_ids, layers, trial_modes, low_edge, high_edge):
    own_rows = trial_modes.shape[0]
    modes_count = trial_modes.shape[1]
    filaments = own_rows * lax.axis_size("fil") * lax.axis_size("col")
    kernel_scale = 1.0 / math.sqrt(filaments)
    own_feats = features(geometry, net_ids, layers)
    row_feat = lax.all_gather(own_feats, "col", axis=1, tiled=True)
    col_feat = lax.all_gather(own_feats, "fil", axis=1, tiled=True)
    tile_rows = row_feat.shape[1]

    def fold_piece(running, gathered):
        length = gathered.shape[0]
        return accumulate(
            running,
            row_feat,
            col_feat,
            gathered,
            kernel_scale,
            column_span(length, tile_rows, own_rows),
        )

    def apply_operator(mode_block):
        initial = jnp.zeros((tile_rows, modes_count), jnp.float32)
        partial_value = fold_piece(initial, lax.all_gather(mode_block, "fil", axis=0, tiled=True))
        summed = lax.psum(partial_value, "col")
        result_rows = lax.dynamic_slice_in_dim(
            summed, lax.axis_index("col") * own_rows, own_rows, 0
        )
        return result_rows

    centre = (low_edge[0] + high_edge[0]) * 0.5
    half_width = (high_edge[0] - low_edge[0]) * 0.5
    filtered_one = (
        (apply_operator(trial_modes) - centre * trial_modes.astype(jnp.float32)) / half_width
    ).astype(jnp.bfloat16)
    second = 2.0 * (
        apply_operator(filtered_one) - centre * filtered_one.astype(jnp.float32)
    ) / half_width - trial_modes.astype(jnp.float32)
    second_low = second.astype(jnp.bfloat16)
    gram_local = jnp.dot(second.T, second, precision=lax.Precision.HIGHEST) / filaments
    image_block = apply_operator(second_low)
    cross_local = jnp.dot(second.T, image_block, precision=lax.Precision.HIGHEST) / filaments
    gram_matrix, cross_matrix = lax.psum((gram_local, cross_local), ("fil", "col"))
    factor = jnp.linalg.cholesky(gram_matrix)
    ritz_basis = jax.scipy.linalg.solve_triangular(factor, second.T, lower=True).T
    half_solved = jax.scipy.linalg.solve_triangular(factor, cross_matrix, lower=True)
    projected = jax.scipy.linalg.solve_triangular(factor, half_solved.T, lower=True).T
    return (ritz_basis, projected)


def solution(mesh):
    in_specs = (
        P(None, ("groups", "fil", "col")),
        P(("groups", "fil", "col")),
        P(("groups", "fil", "col")),
        P(("groups", "fil", "col"), None),
        P("groups"),
        P("groups"),
    )
    out_specs = (P(("groups", "fil", "col"), None), P("groups", None))
    return jax.shard_map(shards, mesh=mesh, in_specs=in_specs, out_specs=out_specs, check_vma=False)
```

profile of v0, /device:TPU:0, one launch (start us, length us, event | category | flops | bytes accessed | tf_op | source)
XLA Modules:
  0.0 248.8 jit_solution(4855814991281380524)
XLA Ops:
  7.2 0.7 slice.162
  7.9 0.7 slice.163
  8.6 0.7 convert_element_type.28
  9.3 0.7 convert_multiply_fusion.1
  10.0 14.8 %all-gather.1 = f32[4,192,8]{1,2,0:T(8,128)S(1)} all-gather(f32[1,192,8]{1,2,0:T(8,128)S(1)} %maximum_bitcast_fusion), channel_id=1, replica_groups=mesh['groups'=2,'fil'=4,'col'=4] {'fil'}, dimensions={0}, use_global_device_ids=true | all-gather | bytes 30720 | tf_op jit(solution)/shard_map/all_gather | solution.py:74
  24.8 5.2 %all-gather = f32[4,192,8]{1,2,0:T(8,128)S(1)} all-gather(f32[1,192,8]{1,2,0:T(8,128)S(1)} %maximum_bitcast_fusion), channel_id=1, replica_groups=mesh['groups'=2,'fil'=4,'col'=4] {'col'}, dimensions={0}, use_global_device_ids=true | all-gather | bytes 30720 | tf_op jit(solution)/shard_map/all_gather | solution.py:73
  30.2 13.3 %all-gather.2 = bf16[4,192,32]{1,2,0:T(8,128)(2,1)S(1)} all-gather(bf16[1,192,32]{1,2,0:T(8,128)(2,1)} %bitcast.57), channel_id=1, replica_groups=mesh['groups'=2,'fil'=4,'col'=4] {'fil'}, dimensions={0}, use_global_device_ids=true | all-gather | bytes 61440 | tf_op jit(solution)/shard_map/all_gather | solution.py:90
  43.8 2.0 multiply_convert_fusion
  45.9 1.1 fusion.13
  48.4 31.1 %all-reduce.5.cloned.1.call-done = f32[768,32]{0,1:T(8,128)} async-done(((f32[768,32]{0,1:T(8,128)}), f32[768,32]{0,1:T(8,128)}) %all-reduce.5.cloned.1.call-update) | async-done | bytes 98320 | tf_op jit(solution)/shard_map/psum | solution.py:91
  79.5 0.9 fusion.2
  80.3 13.2 %all-gather.3 = bf16[4,192,32]{1,2,0:T(8,128)(2,1)S(1)} all-gather(bf16[1,192,32]{1,2,0:T(8,128)(2,1)S(1)} %bitcast.58), channel_id=1, replica_groups=mesh['groups'=2,'fil'=4,'col'=4] {'fil'}, dimensions={0}, use_global_device_ids=true | all-gather | bytes 61440 | tf_op jit(solution)/shard_map/all_gather | solution.py:90
  93.7 1.1 fusion.14
  94.9 31.3 %all-reduce.7.cloned.1.call-done = f32[768,32]{0,1:T(8,128)} async-done(((f32[768,32]{0,1:T(8,128)}), f32[768,32]{0,1:T(8,128)}) %all-reduce.7.cloned.1.call-update) | async-done | bytes 98320 | tf_op jit(solution)/shard_map/psum | solution.py:91
  126.2 0.9 convert_bitcast_fusion
  127.1 13.2 %all-gather.4 = bf16[4,192,32]{1,2,0:T(8,128)(2,1)S(1)} all-gather(bf16[1,192,32]{1,2,0:T(8,128)(2,1)S(1)} %get-tuple-element.81), channel_id=1, replica_groups=mesh['groups'=2,'fil'=4,'col'=4] {'fil'}, dimensions={0}, use_global_device_ids=true | all-gather | bytes 61440 | tf_op jit(solution)/shard_map/all_gather | solution.py:90
  140.5 1.1 fusion.15
  141.8 31.2 %all-reduce.9.cloned.1.call-done = f32[768,32]{0,1:T(8,128)} async-done(((f32[768,32]{0,1:T(8,128)}), f32[768,32]{0,1:T(8,128)}) %all-reduce.9.cloned.1.call-update) | async-done | bytes 98320 | tf_op jit(solution)/shard_map/psum | solution.py:91
  173.0 1.0 convolution_multiply_fusion
  174.1 59.5 %all-reduce = (f32[32,32]{0,1:T(8,128)S(1)}, f32[32,32]{0,1:T(8,128)S(1)}) all-reduce(f32[32,32]{0,1:T(8,128)S(1)} %convolution_multiply_fusion.1, f32[32,32]{0,1:T(8,128)S(1)} %convolution_multiply_fusion), channel_id=1, replica_groups=mesh['groups'=2,'fil'=4,'col'=4] {'fil','col'}, use_global_device_ids=true, to_apply=%region_2.3 | all-reduce | flops 2048 | bytes 16384 | tf_op jit(solution)/shard_map/psum | solution.py:109
  233.6 2.9 %cholesky.16 = f32[32,32]{1,0:T(8,128)S(1)} custom-call(f32[32,32]{1,0:T(8,128)S(1)} %fusion.9), custom_call_target="Cholesky" | custom-call | tf_op jit(solution)/shard_map/jit(cholesky)/cholesky | solution.py:110
  237.9 2.4 custom-call.10
  240.3 0.9 fusion.7
  241.6 0.7 copy.27
  (28 shorter events, 3.0 us)
Async XLA Ops:
  7.2 72.3 %all-reduce.5.cloned.1.call-start = ((), (), s32[]{:S(2)}) async-start(), calls=%async_computation | async-start | bytes 196608 | tf_op jit(solution)/shard_map/psum | solution.py:91
  43.8 35.7 %copy-start = (bf16[192,32]{0,1:T(8,128)(2,1)S(1)}, bf16[192,32]{0,1:T(8,128)(2,1)}, u32[]{:S(2)}) copy-start(bf16[192,32]{0,1:T(8,128)(2,1)} %param.11) | copy-start | bytes 36868
  47.0 79.2 %all-reduce.7.cloned.1.call-start = ((), (), s32[]{:S(2)}) async-start(), calls=%async_computation.1 | async-start | bytes 196608 | tf_op jit(solution)/shard_map/psum | solution.py:91
  94.9 78.1 %all-reduce.9.cloned.1.call-start = ((), (), s32[]{:S(2)}) async-start(), calls=%async_computation.2 | async-start | bytes 196608 | tf_op jit(solution)/shard_map/psum | solution.py:91
Sparse Core Ops, SparseCore 0:
  47.1 32.2 all-reduce.4
  95.0 31.1 all-reduce.6
  141.8 31.1 all-reduce.8
where the time goes:
time: 249 us
  blocking collectives  119 us (48%)
  waiting for transfers between devices  93.6 us (38%)
  between operations  15.1 us (6%)
  other arithmetic  12 us (5%)
  matrix products  5.83 us (2%)
  local copies, waits for them, and re-layouts  2.86 us (1%)
    psum x3, waiting for transfers between devices, apply_operator(): summed = lax.psum(partial_value, 'col')  93.6 us
    psum x1, blocking collectives, shards(): lax.psum((gram_local, cross_local), ('fil', 'col'))  59.5 us
    all_gather x3, blocking collectives, apply_operator(): lax.all_gather(mode_block, 'fil', axis=0, tiled=True)  39.8 us
    all_gather x1, blocking collectives, shards(): col_feat = lax.all_gather(own_feats, 'fil', axis=1, tiled=True)  14.8 us
    all_gather x1, blocking collectives, shards(): row_feat = lax.all_gather(own_feats, 'col', axis=1, tiled=True)  5.18 us
  transfers between devices with their start and end apart: 3, of which 3 were waited for; matrix products, arithmetic and copies ran while one was open for 0% of the time, Pallas kernels for 0%

commit v1 on v0

v1 whole, which is shorter than its diff:
```python
import functools
import math

import jax
import jax.numpy as jnp
from jax import lax
from jax.experimental import pallas as pl
from jax.experimental.pallas import tpu as pltpu
from jax.sharding import PartitionSpec as P

SHIELD_FACTOR = 0.5
LAYER_PITCH = 0.02
NETS = 4
LAYERS = 8
F32 = jnp.float32
BF16 = jnp.bfloat16
HIGHEST = lax.Precision.HIGHEST
VMEM_SPEC = pl.BlockSpec(memory_space=pltpu.VMEM)
SMEM_SPEC = pl.BlockSpec(memory_space=pltpu.SMEM)
PAYLOAD_ROWS = 64
TILE_ROWS = 256
TILE_COLS = 512


def pieces(x):
    high = x.astype(BF16).astype(F32)
    mid = (x - high).astype(BF16).astype(F32)
    low = (x - high - mid).astype(BF16).astype(F32)
    return high, mid, low


def pack_body(geometry, nets, layers, modes, out):
    shape = (1, geometry.shape[1])
    high, mid, low = pieces(geometry[...])
    zeros = jnp.zeros((2,) + shape[1:], F32)
    rest = jnp.zeros((8,) + shape[1:], F32)
    rows = jnp.concatenate(
        [high, nets[...].astype(F32), layers[...].astype(F32), mid, zeros, low, zeros, rest], axis=0
    ).astype(BF16)
    for place in range(out.shape[0]):
        out[place, 0:32, :] = modes[...]
        out[place, 32:64, :] = rows


def tile_body(scale, own, other, low_edge, high_edge, panel, filtered, stage, left, right, coarse, xy, total):
    count, _, width = own.shape
    cols = count * width
    rows = 2 * cols
    for half, part in enumerate((own, other)):
        for place in range(count):
            start = half * cols + place * width
            stage[:, start : start + width] = part[place].astype(F32)

    def rows_of(first, last, length):
        return stage[first:last, 0:length]

    def groups(base, nets):
        listed = [base] + [jnp.where(nets == float(n), base, 0.0) for n in range(NETS)]
        return jnp.concatenate(listed, axis=0)

    def squares(length):
        return pieces(jnp.square(rows_of(37, 38, length) + rows_of(45, 46, length) + rows_of(53, 54, length)))

    nets = rows_of(38, 39, rows)
    segment = [groups(rows_of(s + 2, s + 5, rows), nets) for s in (32, 40, 48)]
    place_x = [rows_of(s, s + 1, rows) for s in (32, 40, 48)]
    place_y = [rows_of(s + 1, s + 2, rows) for s in (32, 40, 48)]
    spare = place_x + place_y
    for index, piece in enumerate((0, 0, 1, 1, 0, 2)):
        left[16 * index : 16 * index + 16, :] = jnp.concatenate([segment[piece], spare[index]], axis=0)
    levels = lax.broadcasted_iota(jnp.int32, (LAYERS, rows), 0).astype(F32)
    chosen = jnp.where(levels == rows_of(39, 40, rows), 1.0, 0.0)
    ones = jnp.ones((3, rows), F32)
    left[96:104, :] = chosen
    left[104:112, :] = chosen
    left[112:120, :] = chosen
    left[120:128, :] = jnp.concatenate([*squares(rows), ones, jnp.zeros((2, rows), F32)], axis=0)

    nets = rows_of(38, 39, cols)
    base = (rows_of(34, 37, cols) + rows_of(42, 45, cols) + rows_of(50, 53, cols)) * (SHIELD_FACTOR * scale)
    scaled = [groups(piece, nets) for piece in pieces(base)]
    blank = jnp.zeros((1, cols), F32)
    for index, piece in enumerate((0, 1, 0, 1, 2, 0)):
        right[16 * index : 16 * index + 16, :] = jnp.concatenate([scaled[piece], blank], axis=0).astype(BF16)
    right[96:128, :] = jnp.zeros((32, cols), BF16)
    coarse[0:96, :] = jnp.zeros((96, cols), BF16)
    levels = lax.broadcasted_iota(jnp.int32, (LAYERS, cols), 0).astype(F32)
    gap = levels * LAYER_PITCH - rows_of(39, 40, cols) * LAYER_PITCH
    ones = jnp.ones((3, cols), F32)
    coarse[96:128, :] = jnp.concatenate(
        [*pieces(gap * gap), ones, *squares(cols), jnp.zeros((2, cols), F32)], axis=0
    ).astype(BF16)
    own_x = rows_of(32, 33, cols) + rows_of(40, 41, cols) + rows_of(48, 49, cols)
    own_y = rows_of(33, 34, cols) + rows_of(41, 42, cols) + rows_of(49, 50, cols)
    line = lax.broadcasted_iota(jnp.int32, (128, 256), 0)
    lane = lax.broadcasted_iota(jnp.int32, (128, 256), 1)
    for_x = (lane < 128) & ((line == 15) | (line == 31) | (line == 47))
    for_y = (lane >= 128) & ((line == 63) | (line == 79) | (line == 95))
    xy[...] = jnp.where(for_x | for_y, 1.0, 0.0).astype(BF16)

    total[...] = jnp.zeros_like(total)

    def step(turn, carry):
        start = pl.multiple_of(turn * TILE_ROWS, TILE_ROWS)
        feats = left[:, pl.ds(start, TILE_ROWS)].T.astype(BF16)
        places = jnp.dot(feats, xy[...], preferred_element_type=F32)
        modes = stage[0:32, pl.ds(start, TILE_ROWS)].astype(BF16)
        tall_x = jnp.concatenate([places[:, 0:128]] * (TILE_COLS // 128), axis=1)
        tall_y = jnp.concatenate([places[:, 128:256]] * (TILE_COLS // 128), axis=1)
        for first in range(0, cols, TILE_COLS):
            here = slice(first, first + TILE_COLS)
            aligned = jnp.dot(feats, right[:, here], preferred_element_type=F32)
            spread = jnp.dot(feats, coarse[:, here], preferred_element_type=F32)
            delta_x = tall_x - own_x[:, here]
            delta_y = tall_y - own_y[:, here]
            spread = delta_x * delta_x + delta_y * delta_y + spread
            tile = (aligned * lax.rsqrt(spread)).astype(BF16)
            panel[pl.ds(start, TILE_ROWS), here] = tile
            total[:, here] += jnp.dot(modes, tile, preferred_element_type=F32)
        return carry

    lax.fori_loop(0, rows // TILE_ROWS, step, 0)
    centre = (low_edge[0] + high_edge[0]) * 0.5
    half_width = (high_edge[0] - low_edge[0]) * 0.5
    filtered[...] = ((total[...] - centre * stage[0:32, 0:cols]) / half_width).astype(BF16)


def product(panel, own, other):
    cols = own.shape[1]
    return jnp.dot(own[...], panel[0:cols, :], preferred_element_type=F32) + jnp.dot(
        other[...], panel[cols : 2 * cols, :], preferred_element_type=F32
    )


def second_body(panel, own, other, modes, low_edge, high_edge, second, second_low):
    count, _, width = modes.shape
    applied = product(panel, own, other)
    centre = (low_edge[0] + high_edge[0]) * 0.5
    half_width = (high_edge[0] - low_edge[0]) * 0.5
    second[...] = 2.0 * (applied - centre * own[...].astype(F32)) / half_width
    for place in range(count):
        here = slice(place * width, place * width + width)
        second[:, here] = second[:, here] - modes[place, 0:32, :].astype(F32)
    second_low[...] = second[...].astype(BF16)


def image_body(filaments, panel, own, other, second, sums):
    applied = product(panel, own, other)
    block = second[...]
    zeros = jnp.zeros_like(block)
    stacked = jnp.concatenate([block, zeros, applied, zeros], axis=0)
    sums[...] = (
        lax.dot_general(block, stacked, (((1,), (1,)), ((), ())), precision=HIGHEST, preferred_element_type=F32)
        / filaments
    )


def ritz_body(axes, sums, sums_other, second, ritz, projected):
    modes, width = ritz.shape
    line = lax.broadcasted_iota(jnp.int32, (modes, 128), 0)
    lane = lax.broadcasted_iota(jnp.int32, (modes, 128), 1)
    system = sums[...] + sums_other[...] + jnp.where(lane == line + modes, 1.0, 0.0)
    for pivot in range(modes):
        row = system[pivot : pivot + 1, :]
        column = system[:, pivot : pivot + 1] / system[pivot : pivot + 1, pivot : pivot + 1]
        column = jnp.where(line[:, 0:1] > pivot, column, 0.0)
        system = system - column * row
    diagonal = jnp.sum(jnp.where(lane == line, system, 0.0), axis=1, keepdims=True)
    system = system / jnp.sqrt(diagonal)
    inverse = system[:, modes : 2 * modes]
    half_solved = system[:, 2 * modes : 3 * modes]
    projected[...] = lax.dot_general(
        half_solved, inverse, (((1,), (1,)), ((), ())), precision=HIGHEST, preferred_element_type=F32
    )
    fil, col, col_size = axes
    place = lax.axis_index(fil) * (col_size // 2) + lax.axis_index(col) // 2
    if width % 128 == 0:
        mine = second[:, pl.ds(pl.multiple_of(place * width, 128), width)]
    else:
        odd = place % 2
        start = (place // 2) * (2 * width) + odd * (width - 64)
        window = second[:, pl.ds(pl.multiple_of(start, 128), width + 64)]
        moved = pltpu.roll(window, width, 1)
        mine = jnp.where(odd == 1, moved, window)[:, 0:width]
    ritz[...] = jnp.dot(inverse, mine, precision=HIGHEST, preferred_element_type=F32)


def call(body, name, out_shape, in_specs, scratch=(), limit=16):
    return pl.pallas_call(
        body,
        name=name,
        out_shape=out_shape,
        in_specs=in_specs,
        out_specs=jax.tree.map(lambda _: VMEM_SPEC, out_shape),
        scratch_shapes=list(scratch),
        compiler_params=pltpu.CompilerParams(vmem_limit_bytes=limit * 1024 * 1024),
    )


def paired_shards(geometry, net_ids, layers, trial_modes, low_edge, high_edge):
    width, modes = trial_modes.shape
    fil, col = lax.axis_size("fil"), lax.axis_size("col")
    count = fil * col // 2
    cols = count * width
    rows = 2 * cols
    shape = jax.ShapeDtypeStruct
    pair = [(i, i ^ 1) for i in range(col)]
    same_core = [[2 * chip + core for chip in range(count)] for core in range(2)]

    packed = call(pack_body, "pack", shape((count, PAYLOAD_ROWS, width), BF16), [VMEM_SPEC] * 4)(
        geometry, net_ids.reshape(1, width), layers.reshape(1, width), trial_modes.T
    )
    own = lax.all_to_all(packed, ("fil", "col"), 0, 0, axis_index_groups=same_core, tiled=True)
    other = lax.ppermute(own, "col", pair)
    panel, filtered = call(
        functools.partial(tile_body, 1.0 / math.sqrt(rows)),
        "tiles",
        (pltpu.VMEM((rows, cols), BF16), shape((modes, cols), BF16)),
        [VMEM_SPEC] * 2 + [SMEM_SPEC] * 2,
        [
            pltpu.VMEM((PAYLOAD_ROWS, rows), F32),
            pltpu.VMEM((128, rows), F32),
            pltpu.VMEM((128, cols), BF16),
            pltpu.VMEM((128, cols), BF16),
            pltpu.VMEM((128, 256), BF16),
            pltpu.VMEM((modes, cols), F32),
        ],
        limit=32,
    )(own, other, low_edge, high_edge)
    second, second_low = call(
        second_body,
        "second",
        (shape((modes, cols), F32), shape((modes, cols), BF16)),
        [VMEM_SPEC] * 4 + [SMEM_SPEC] * 2,
    )(panel, filtered, lax.ppermute(filtered, "col", pair), own, low_edge, high_edge)
    sums = call(functools.partial(image_body, float(rows)), "image", shape((modes, 128), F32), [VMEM_SPEC] * 4)(
        panel, second_low, lax.ppermute(second_low, "col", pair), second
    )
    ritz, projected = call(
        functools.partial(ritz_body, ("fil", "col", col)),
        "ritz",
        (shape((modes, width), F32), shape((modes, modes), F32)),
        [VMEM_SPEC] * 3,
    )(sums, lax.ppermute(sums, "col", pair), second)
    return ritz.T, projected


def features(geometry, net_ids, layers):
    height = layers.astype(F32) * LAYER_PITCH
    return jnp.concatenate([geometry[0:2], height[None], geometry[2:6], net_ids.astype(F32)[None]], axis=0)


def kernel_tile(row_feat, col_feat, kernel_scale):
    delta_x = row_feat[0][:, None] - col_feat[0][None, :]
    delta_y = row_feat[1][:, None] - col_feat[1][None, :]
    delta_z = row_feat[2][:, None] - col_feat[2][None, :]
    radius_sq = (
        row_feat[6][:, None] * row_feat[6][:, None] + col_feat[6][None, :] * col_feat[6][None, :]
    )
    spread = delta_x * delta_x + delta_y * delta_y + delta_z * delta_z + radius_sq
    alignment = (
        row_feat[3][:, None] * col_feat[3][None, :]
        + row_feat[4][:, None] * col_feat[4][None, :]
        + row_feat[5][:, None] * col_feat[5][None, :]
    )
    couple = jnp.where(row_feat[7][:, None] == col_feat[7][None, :], 1.0, SHIELD_FACTOR)
    return (alignment * couple * lax.rsqrt(spread) * kernel_scale).astype(BF16)


def column_span(length, tile_rows, shard_rows):
    span_limit = max(shard_rows, (1 << 20) // tile_rows)
    span_cols = shard_rows
    while span_cols * 2 <= span_limit and length % (span_cols * 2) == 0:
        span_cols = span_cols * 2
    return span_cols


def accumulate(running, row_feat, part_feats, gathered, kernel_scale, span_cols):
    turns = gathered.shape[0] // span_cols

    def one_span(turn_index, partial_sum):
        offset = turn_index * span_cols
        span_feats = lax.dynamic_slice_in_dim(part_feats, offset, span_cols, 1)
        span_modes = lax.dynamic_slice_in_dim(gathered, offset, span_cols, 0)
        tile_vals = kernel_tile(row_feat, span_feats, kernel_scale)
        return partial_sum + jnp.dot(tile_vals, span_modes, preferred_element_type=F32)

    return lax.fori_loop(0, turns, one_span, running)


def general_shards(geometry, net_ids, layers, trial_modes, low_edge, high_edge):
    own_rows, modes_count = trial_modes.shape
    filaments = own_rows * lax.axis_size("fil") * lax.axis_size("col")
    kernel_scale = 1.0 / math.sqrt(filaments)
    own_feats = features(geometry, net_ids, layers)
    row_feat = lax.all_gather(own_feats, "col", axis=1, tiled=True)
    col_feat = lax.all_gather(own_feats, "fil", axis=1, tiled=True)
    tile_rows = row_feat.shape[1]

    def apply_operator(mode_block):
        gathered = lax.all_gather(mode_block, "fil", axis=0, tiled=True)
        initial = jnp.zeros((tile_rows, modes_count), F32)
        span = column_span(gathered.shape[0], tile_rows, own_rows)
        partial_value = accumulate(initial, row_feat, col_feat, gathered, kernel_scale, span)
        summed = lax.psum(partial_value, "col")
        return lax.dynamic_slice_in_dim(summed, lax.axis_index("col") * own_rows, own_rows, 0)

    centre = (low_edge[0] + high_edge[0]) * 0.5
    half_width = (high_edge[0] - low_edge[0]) * 0.5
    filtered_one = (
        (apply_operator(trial_modes) - centre * trial_modes.astype(F32)) / half_width
    ).astype(BF16)
    second = 2.0 * (
        apply_operator(filtered_one) - centre * filtered_one.astype(F32)
    ) / half_width - trial_modes.astype(F32)
    second_low = second.astype(BF16)
    gram_local = jnp.dot(second.T, second, precision=HIGHEST) / filaments
    image_block = apply_operator(second_low)
    cross_local = jnp.dot(second.T, image_block, precision=HIGHEST) / filaments
    gram_matrix, cross_matrix = lax.psum((gram_local, cross_local), ("fil", "col"))
    factor = jnp.linalg.cholesky(gram_matrix)
    ritz_basis = jax.scipy.linalg.solve_triangular(factor, second.T, lower=True).T
    half_solved = jax.scipy.linalg.solve_triangular(factor, cross_matrix, lower=True)
    projected = jax.scipy.linalg.solve_triangular(factor, half_solved.T, lower=True).T
    return (ritz_basis, projected)


def fits(mesh, width, modes):
    count = mesh.shape["fil"] * mesh.shape["col"]
    rows = count * width
    return (
        mesh.shape["col"] % 2 == 0
        and (count // 2) % 2 == 0
        and modes == 32
        and width % 64 == 0
        and (rows // 2) % TILE_COLS == 0
        and rows % TILE_ROWS == 0
        and rows * rows <= 16 * 1024 * 1024
    )


def solution(mesh):
    in_specs = (
        P(None, ("groups", "fil", "col")),
        P(("groups", "fil", "col")),
        P(("groups", "fil", "col")),
        P(("groups", "fil", "col"), None),
        P("groups"),
        P("groups"),
    )
    out_specs = (P(("groups", "fil", "col"), None), P("groups", None))

    def shards(geometry, net_ids, layers, trial_modes, low_edge, high_edge):
        form = paired_shards if fits(mesh, *trial_modes.shape) else general_shards
        return form(geometry, net_ids, layers, trial_modes, low_edge, high_edge)

    return jax.shard_map(shards, mesh=mesh, in_specs=in_specs, out_specs=out_specs, check_vma=False)
```

time: 249 us -> 47 us (0.19)
  blocking collectives: 119 us -> 16 us
  waiting for transfers between devices: 93.6 us -> 3.15 us
  Pallas kernels: 0 us -> 21.8 us
  between operations: 15.1 us -> 1.96 us
  other arithmetic: 12 us -> 0 us
  matrix products: 5.83 us -> 0 us
    psum x3 -> x0, waiting for transfers between devices: 93.6 us -> none  [apply_operator(): summed = lax.psum(partial_value, 'col')]
    all_gather x5 -> x0, blocking collectives: 59.8 us -> none  [the longest x3 39.8 us: apply_operator(): lax.all_gather(mode_block, 'fil', axis=0, tiled=True)]
    psum x1 -> x0, blocking collectives: 59.5 us -> none  [shards(): lax.psum((gram_local, cross_local), ('fil', 'col'))]
    pallas_call x0 -> x5, Pallas kernels: none -> 21.8 us  [the longest x1 14.1 us: paired_shards(): call(functools.partial(tile_body, 1.0 / math.sqrt(rows)), 'tiles', (pltpu...]
    all_to_all x0 -> x1, blocking collectives: none -> 16 us  [paired_shards(): lax.all_to_all(packed, ('fil', 'col'), 0, 0, axis_index_groups=same_core,...]
    another operation x5 -> x0, other arithmetic: 6.68 us -> none  [the longest x3 3.59 us: shards(): factor = jnp.linalg.cholesky(gram_matrix)]
    dot_general x5 -> x0, matrix products: 4.56 us -> none  [the longest x3 3.37 us: one_span(): jnp.dot(tile_vals, span_modes, preferred_element_type=jnp.float32)]
    convert_element_type x3 -> x0, other arithmetic: 3.61 us -> none  [the longest x1 2.05 us: kernel_tile(): (alignment * couple * lax.rsqrt(spread) * kernel_scale).astype(jnp.bfloat16)]
  transfers between devices with their start and end apart: 3 -> 4, of which waited for: 3 -> 4; matrix products, arithmetic and copies ran while one was open for 0% -> 0% of each run, Pallas kernels for 0% -> 0%
where the time goes in v1:
time: 47 us; the launch traced here: 46.7 us
  Pallas kernels  21.8 us (46%)
  blocking collectives  16 us (34%)
  waiting for transfers between devices  3.15 us (7%)
  local copies, waits for them, and re-layouts  2.76 us (6%)
  between operations  1.96 us (4%)
  starting transfers between devices  1.03 us (2%)
    all_to_all x1, blocking collectives, paired_shards(): lax.all_to_all(packed, ('fil', 'col'), 0, 0, axis_index_groups=same_core,...  16 us
    pallas_call x1, Pallas kernels, paired_shards(): call(functools.partial(tile_body, 1.0 / math.sqrt(rows)), 'tiles', (pltpu...  14.1 us
    pallas_call x1, Pallas kernels, paired_shards(): call(functools.partial(ritz_body, ('fil', 'col', col)), 'ritz', (shape((m...  3.47 us
    unnamed x8, local copies, waits for them, and re-layouts  2.76 us
    pallas_call x1, Pallas kernels, paired_shards(): call(functools.partial(image_body, float(rows)), 'image', shape((modes, 1...  2.47 us
    pallas_call x1, Pallas kernels, paired_shards(): call(second_body, 'second', (shape((modes, cols), F32), shape((modes, col...  1.74 us
    ppermute x1, waiting for transfers between devices, paired_shards(): lax.ppermute(filtered, 'col', pair)  1.01 us
    ppermute x1, waiting for transfers between devices, paired_shards(): lax.ppermute(second_low, 'col', pair)  1.01 us
  transfers between devices with their start and end apart: 4, of which 4 were waited for; matrix products, arithmetic and copies ran while one was open for 0% of the time, Pallas kernels for 0%

profile of v1, /device:TPU:0, one launch (start us, length us, event | category | flops | bytes accessed | tf_op | source)
XLA Modules:
  0.0 46.7 jit_solution(16366517737296983781)
XLA Ops:
  0.6 0.0 copy-start
  0.6 0.7 %copy-done = bf16[192,32]{0,1:T(8,128)(2,1)S(1)} copy-done((bf16[192,32]{0,1:T(8,128)(2,1)S(1)}, bf16[192,32]{0,1:T(8,128)(2,1)}, u32[]{:S(2)}) %copy-start) | copy-done | bytes 12312
  1.3 0.0 copy-start.1
  1.4 0.7 %copy-done.1 = f32[6,192]{1,0:T(8,128)S(1)} copy-done((f32[6,192]{1,0:T(8,128)S(1)}, f32[6,192]{1,0:T(8,128)}, u32[]{:S(2)}) %copy-start.1) | copy-done | bytes 4632
  2.0 0.0 copy-start.2
  2.0 0.7 %copy-done.2 = s32[192]{0:T(256)S(1)} copy-done((s32[192]{0:T(256)S(1)}, s32[192]{0:T(256)}, u32[]{:S(2)}) %copy-start.2) | copy-done | bytes 792
  2.7 0.0 copy-start.3
  2.7 0.7 %copy-done.3 = s32[192]{0:T(256)S(1)} copy-done((s32[192]{0:T(256)S(1)}, s32[192]{0:T(256)}, u32[]{:S(2)}) %copy-start.3) | copy-done | bytes 792
  3.4 16.0 %all_to_all.5.own.modes = bf16[8,64,192]{2,1,0:T(8,128)(2,1)S(1)} all-to-all(bf16[8,64,192]{2,1,0:T(8,128)(2,1)S(1)} %pack.1), channel_id=1, replica_groups={{0,2,4,6,8,10,12,14},{1,3,5,7,9,11,13,15},{16,18,20,22,24,26,28,30},{17..., dimensions={0} | all-to-all | bytes 393216 | tf_op jit(solution)/shard_map/all_to_all | solution.py:213
  19.4 0.0 collective-permute-start
  20.7 0.2 collective-permute-done.other
  20.9 14.1 %tiles.1 = (bf16[3072,1536]{1,0:T(8,128)(2,1)S(1)}, bf16[32,1536]{1,0:T(8,128)(2,1)S(1)}) custom-call(bf16[8,64,192]{2,1,0:T(8,128)(2,1)S(1)} %all_to_all.5.own.modes, bf16[8,64,192]{2,1,0:T(8,128)(2,1)S(1)} %collective-permute-done.other, f32[1]{0:T(128)S(6)} %copy.8.low_edge, f32[1]{0:T(128)S(6)} %copy.9.high_edge), custom_call_target="tpu_custom_call" | custom-call | tf_op jit(solution)/shard_map/tiles/pallas_call | solution.py:215
  35.0 0.4 collective-permute-start.1
  35.4 1.0 %collective-permute-done.1.other = bf16[32,1536]{1,0:T(8,128)(2,1)S(1)} collective-permute-done((bf16[32,1536]{1,0:T(8,128)(2,1)S(1)}, bf16[32,1536]{1,0:T(8,128)(2,1)S(1)}, u32[]{:S(2)}, u32[]{:S(2)}) %collective-permute-start.1) | collective-permute-done | bytes 98336 | tf_op jit(solution)/shard_map/ppermute | solution.py:235
  36.4 1.7 %second.1 = (f32[32,1536]{1,0:T(8,128)S(1)}, bf16[32,1536]{1,0:T(8,128)(2,1)S(1)}) custom-call(bf16[3072,1536]{1,0:T(8,128)(2,1)S(1)} %get-tuple-element.8.panel, bf16[32,1536]{1,0:T(8,128)(2,1)S(1)} %get-tuple-element.9.own, bf16[32,1536]{1,0:T(8,128)(2,1)S(1)} %collective-permute-done.1.other, bf16[8,64,192]{2,1,0:T(8,128)(2,1)S(1)} %all_to_all.5.own.modes, ...), custom_call_target="tpu_custom_call" | custom-call | tf_op jit(solution)/shard_map/second/pallas_call | solution.py:230
  38.2 0.4 collective-permute-start.2
  38.5 1.0 %collective-permute-done.2.other = bf16[32,1536]{1,0:T(8,128)(2,1)S(1)} collective-permute-done((bf16[32,1536]{1,0:T(8,128)(2,1)S(1)}, bf16[32,1536]{1,0:T(8,128)(2,1)S(1)}, u32[]{:S(2)}, u32[]{:S(2)}) %collective-permute-start.2) | collective-permute-done | bytes 98336 | tf_op jit(solution)/shard_map/ppermute | solution.py:237
  39.5 2.5 %image.1.sums = f32[32,128]{1,0:T(8,128)S(1)} custom-call(bf16[3072,1536]{1,0:T(8,128)(2,1)S(1)} %get-tuple-element.8.panel, bf16[32,1536]{1,0:T(8,128)(2,1)S(1)} %get-tuple-element.10.own, bf16[32,1536]{1,0:T(8,128)(2,1)S(1)} %collective-permute-done.2.other, f32[32,1536]{1,0:T(8,128)S(1)} %get-tuple-element.11.second), custom_call_target="tpu_custom_call" | custom-call | tf_op jit(solution)/shard_map/image/pallas_call | solution.py:236
  42.0 0.3 collective-permute-start.3
  42.3 0.9 %collective-permute-done.3.sums_other = f32[32,128]{1,0:T(8,128)S(1)} collective-permute-done((f32[32,128]{1,0:T(8,128)S(1)}, f32[32,128]{1,0:T(8,128)S(1)}, u32[]{:S(2)}, u32[]{:S(2)}) %collective-permute-start.3) | collective-permute-done | bytes 16416 | tf_op jit(solution)/shard_map/ppermute | solution.py:244
  43.2 3.5 %ritz.1 = (f32[32,192]{1,0:T(8,128)}, f32[32,32]{1,0:T(8,128)}) custom-call(f32[32,128]{1,0:T(8,128)S(1)} %image.1.sums, f32[32,128]{1,0:T(8,128)S(1)} %collective-permute-done.3.sums_other, f32[32,1536]{1,0:T(8,128)S(1)} %get-tuple-element.11.second), custom_call_target="tpu_custom_call" | custom-call | tf_op jit(solution)/shard_map/ritz/pallas_call | solution.py:239
  (1 shorter events, 0.0 us)
Async XLA Ops:
  0.6 0.7 %copy-start = (bf16[192,32]{0,1:T(8,128)(2,1)S(1)}, bf16[192,32]{0,1:T(8,128)(2,1)}, u32[]{:S(2)}) copy-start(bf16[192,32]{0,1:T(8,128)(2,1)} %param.9) | copy-start | bytes 36868
  1.3 0.7 %copy-start.1 = (f32[6,192]{1,0:T(8,128)S(1)}, f32[6,192]{1,0:T(8,128)}, u32[]{:S(2)}) copy-start(f32[6,192]{1,0:T(8,128)} %geometry.1) | copy-start | bytes 13828
  2.0 0.7 %copy-start.2 = (s32[192]{0:T(256)S(1)}, s32[192]{0:T(256)}, u32[]{:S(2)}) copy-start(s32[192]{0:T(256)} %param.7) | copy-start | bytes 2308
  2.7 0.7 %copy-start.3 = (s32[192]{0:T(256)S(1)}, s32[192]{0:T(256)}, u32[]{:S(2)}) copy-start(s32[192]{0:T(256)} %param.8) | copy-start | bytes 2308
  19.4 1.5 %collective-permute-start = (bf16[8,64,192]{2,1,0:T(8,128)(2,1)S(1)}, bf16[8,64,192]{2,1,0:T(8,128)(2,1)S(1)}, u32[]{:S(2)}, u32[]{:S(2)}) collective-permute-start(bf16[8,64,192]{2,1,0:T(8,128)(2,1)S(1)} %all_to_all.5.own.modes), channel_id=1, source_target_pairs={{0,1},{1,0},{2,3},{3,2},{4,5},{5,4},{6,7},{7,6},{8,9},{9,8},{10,11... | collective-permute-start | bytes 589832 | tf_op jit(solution)/shard_map/ppermute | solution.py:214
  35.0 1.4 %collective-permute-start.1 = (bf16[32,1536]{1,0:T(8,128)(2,1)S(1)}, bf16[32,1536]{1,0:T(8,128)(2,1)S(1)}, u32[]{:S(2)}, u32[]{:S(2)}) collective-permute-start(bf16[32,1536]{1,0:T(8,128)(2,1)S(1)} %get-tuple-element.9.own), channel_id=1, source_target_pairs={{0,1},{1,0},{2,3},{3,2},{4,5},{5,4},{6,7},{7,6},{8,9},{9,8},{10,11... | collective-permute-start | bytes 294920 | tf_op jit(solution)/shard_map/ppermute | solution.py:235
  38.2 1.4 %collective-permute-start.2 = (bf16[32,1536]{1,0:T(8,128)(2,1)S(1)}, bf16[32,1536]{1,0:T(8,128)(2,1)S(1)}, u32[]{:S(2)}, u32[]{:S(2)}) collective-permute-start(bf16[32,1536]{1,0:T(8,128)(2,1)S(1)} %get-tuple-element.10.own), channel_id=1, source_target_pairs={{0,1},{1,0},{2,3},{3,2},{4,5},{5,4},{6,7},{7,6},{8,9},{9,8},{10,11... | collective-permute-start | bytes 294920 | tf_op jit(solution)/shard_map/ppermute | solution.py:237
  42.0 1.2 %collective-permute-start.3 = (f32[32,128]{1,0:T(8,128)S(1)}, f32[32,128]{1,0:T(8,128)S(1)}, u32[]{:S(2)}, u32[]{:S(2)}) collective-permute-start(f32[32,128]{1,0:T(8,128)S(1)} %image.1.sums), channel_id=1, source_target_pairs={{0,1},{1,0},{2,3},{3,2},{4,5},{5,4},{6,7},{7,6},{8,9},{9,8},{10,11... | collective-permute-start | bytes 49160 | tf_op jit(solution)/shard_map/ppermute | solution.py:244

commit v2 on v1

--- a/solution.py
+++ b/solution.py
@@ -18,8 +18,8 @@
 VMEM_SPEC = pl.BlockSpec(memory_space=pltpu.VMEM)
 SMEM_SPEC = pl.BlockSpec(memory_space=pltpu.SMEM)
 PAYLOAD_ROWS = 64
-TILE_ROWS = 256
-TILE_COLS = 512
+TILE_ROWS = 512
+TILE_COLS = 256
 
 
 def pieces(x):
@@ -42,10 +42,11 @@
         out[place, 32:64, :] = rows
 
 
-def tile_body(scale, own, other, low_edge, high_edge, panel, filtered, stage, left, right, coarse, xy, total):
+def tile_body(scale, own, other, low_edge, high_edge, panel_own, panel_other, filtered, stage, left, right, coarse, xy, total):
     count, _, width = own.shape
     cols = count * width
     rows = 2 * cols
+    panels = (panel_own, panel_other)
     for half, part in enumerate((own, other)):
         for place in range(count):
             start = half * cols + place * width
@@ -100,11 +101,12 @@
 
     total[...] = jnp.zeros_like(total)
 
-    def step(turn, carry):
-        start = pl.multiple_of(turn * TILE_ROWS, TILE_ROWS)
+    def generate(half, turn):
+        near = pl.multiple_of(turn * TILE_ROWS, TILE_ROWS)
+        start = pl.multiple_of(half * cols + turn * TILE_ROWS, TILE_ROWS)
+        panel = panels[half]
         feats = left[:, pl.ds(start, TILE_ROWS)].T.astype(BF16)
         places = jnp.dot(feats, xy[...], preferred_element_type=F32)
-        modes = stage[0:32, pl.ds(start, TILE_ROWS)].astype(BF16)
         tall_x = jnp.concatenate([places[:, 0:128]] * (TILE_COLS // 128), axis=1)
         tall_y = jnp.concatenate([places[:, 128:256]] * (TILE_COLS // 128), axis=1)
         for first in range(0, cols, TILE_COLS):
@@ -114,27 +116,42 @@
             delta_x = tall_x - own_x[:, here]
             delta_y = tall_y - own_y[:, here]
             spread = delta_x * delta_x + delta_y * delta_y + spread
-            tile = (aligned * lax.rsqrt(spread)).astype(BF16)
-            panel[pl.ds(start, TILE_ROWS), here] = tile
-            total[:, here] += jnp.dot(modes, tile, preferred_element_type=F32)
+            panel[pl.ds(near, TILE_ROWS), here] = (aligned * lax.rsqrt(spread)).astype(BF16)
+
+    def multiply(half, turn):
+        near = pl.multiple_of(turn * TILE_ROWS, TILE_ROWS)
+        start = pl.multiple_of(half * cols + turn * TILE_ROWS, TILE_ROWS)
+        modes = stage[0:32, pl.ds(start, TILE_ROWS)].astype(BF16)
+        total[...] += jnp.dot(modes, panels[half][pl.ds(near, TILE_ROWS), :], preferred_element_type=F32)
+
+    generate(0, 0)
+
+    def step(turn, carry):
+        multiply(0, turn)
+        generate(1, turn)
+        multiply(1, turn)
+        generate(0, turn + 1)
         return carry
 
-    lax.fori_loop(0, rows // TILE_ROWS, step, 0)
+    last = cols // TILE_ROWS - 1
+    lax.fori_loop(0, last, step, 0)
+    multiply(0, last)
+    generate(1, last)
+    multiply(1, last)
     centre = (low_edge[0] + high_edge[0]) * 0.5
     half_width = (high_edge[0] - low_edge[0]) * 0.5
     filtered[...] = ((total[...] - centre * stage[0:32, 0:cols]) / half_width).astype(BF16)
 
 
-def product(panel, own, other):
-    cols = own.shape[1]
-    return jnp.dot(own[...], panel[0:cols, :], preferred_element_type=F32) + jnp.dot(
-        other[...], panel[cols : 2 * cols, :], preferred_element_type=F32
-    )
-
-
-def second_body(panel, own, other, modes, low_edge, high_edge, second, second_low):
+def product(panel_own, panel_other, own, other):
+    return jnp.dot(own[...], panel_own[...], preferred_element_type=F32) + jnp.dot(
+        other[...], panel_other[...], preferred_element_type=F32
+    )
+
+
+def second_body(panel_own, panel_other, own, other, modes, low_edge, high_edge, second, second_low):
     count, _, width = modes.shape
-    applied = product(panel, own, other)
+    applied = product(panel_own, panel_other, own, other)
     centre = (low_edge[0] + high_edge[0]) * 0.5
     half_width = (high_edge[0] - low_edge[0]) * 0.5
     second[...] = 2.0 * (applied - centre * own[...].astype(F32)) / half_width
@@ -144,8 +161,8 @@
     second_low[...] = second[...].astype(BF16)
 
 
-def image_body(filaments, panel, own, other, second, sums):
-    applied = product(panel, own, other)
+def image_body(filaments, panel_own, panel_other, own, other, second, sums):
+    applied = product(panel_own, panel_other, own, other)
     block = second[...]
     zeros = jnp.zeros_like(block)
     stacked = jnp.concatenate([block, zeros, applied, zeros], axis=0)
@@ -212,10 +229,10 @@
     )
     own = lax.all_to_all(packed, ("fil", "col"), 0, 0, axis_index_groups=same_core, tiled=True)
     other = lax.ppermute(own, "col", pair)
-    panel, filtered = call(
+    panel_own, panel_other, filtered = call(
         functools.partial(tile_body, 1.0 / math.sqrt(rows)),
         "tiles",
-        (pltpu.VMEM((rows, cols), BF16), shape((modes, cols), BF16)),
+        (pltpu.VMEM((cols, cols), BF16), pltpu.VMEM((cols, cols), BF16), shape((modes, cols), BF16)),
         [VMEM_SPEC] * 2 + [SMEM_SPEC] * 2,
         [
             pltpu.VMEM((PAYLOAD_ROWS, rows), F32),
@@ -231,10 +248,10 @@
         second_body,
         "second",
         (shape((modes, cols), F32), shape((modes, cols), BF16)),
-        [VMEM_SPEC] * 4 + [SMEM_SPEC] * 2,
-    )(panel, filtered, lax.ppermute(filtered, "col", pair), own, low_edge, high_edge)
-    sums = call(functools.partial(image_body, float(rows)), "image", shape((modes, 128), F32), [VMEM_SPEC] * 4)(
-        panel, second_low, lax.ppermute(second_low, "col", pair), second
+        [VMEM_SPEC] * 5 + [SMEM_SPEC] * 2,
+    )(panel_own, panel_other, filtered, lax.ppermute(filtered, "col", pair), own, low_edge, high_edge)
+    sums = call(functools.partial(image_body, float(rows)), "image", shape((modes, 128), F32), [VMEM_SPEC] * 5)(
+        panel_own, panel_other, second_low, lax.ppermute(second_low, "col", pair), second
     )
     ritz, projected = call(
         functools.partial(ritz_body, ("fil", "col", col)),
@@ -334,7 +351,7 @@
         and modes == 32
         and width % 64 == 0
         and (rows // 2) % TILE_COLS == 0
-        and rows % TILE_ROWS == 0
+        and (rows // 2) % TILE_ROWS == 0
         and rows * rows <= 16 * 1024 * 1024
     )
 

time: 47 us -> 41.3 us (0.88)
  Pallas kernels: 21.8 us -> 16 us
    pallas_call x1, Pallas kernels: 14.1 us -> 8.32 us  [paired_shards(): call(functools.partial(tile_body, 1.0 / math.sqrt(rows)), 'tiles', (pltpu...]
where the time goes in v2:
time: 41.3 us; the launch traced here: 40.9 us
  Pallas kernels  16 us (39%)
  blocking collectives  16 us (39%)
  waiting for transfers between devices  3.16 us (8%)
  local copies, waits for them, and re-layouts  2.76 us (7%)
  between operations  1.96 us (5%)
  starting transfers between devices  1.01 us (2%)
    all_to_all x1, blocking collectives, paired_shards(): lax.all_to_all(packed, ('fil', 'col'), 0, 0, axis_index_groups=same_core,...  16 us
    pallas_call x1, Pallas kernels, paired_shards(): call(functools.partial(tile_body, 1.0 / math.sqrt(rows)), 'tiles', (pltpu...  8.32 us
    pallas_call x1, Pallas kernels, paired_shards(): call(functools.partial(ritz_body, ('fil', 'col', col)), 'ritz', (shape((m...  3.47 us
    unnamed x8, local copies, waits for them, and re-layouts  2.76 us
    pallas_call x1, Pallas kernels, paired_shards(): call(functools.partial(image_body, float(rows)), 'image', shape((modes, 1...  2.48 us
    pallas_call x1, Pallas kernels, paired_shards(): call(second_body, 'second', (shape((modes, cols), F32), shape((modes, col...  1.74 us
    ppermute x1, waiting for transfers between devices, paired_shards(): lax.ppermute(filtered, 'col', pair)  1.02 us
    ppermute x1, waiting for transfers between devices, paired_shards(): lax.ppermute(second_low, 'col', pair)  1.01 us
  transfers between devices with their start and end apart: 4, of which 4 were waited for; matrix products, arithmetic and copies ran while one was open for 0% of the time, Pallas kernels for 0%

profile of v2, /device:TPU:0, one launch (start us, length us, event | category | flops | bytes accessed | tf_op | source)
XLA Modules:
  0.0 40.9 jit_solution(13079358082678702276)
XLA Ops:
  0.6 0.0 copy-start
  0.6 0.7 %copy-done = bf16[192,32]{0,1:T(8,128)(2,1)S(1)} copy-done((bf16[192,32]{0,1:T(8,128)(2,1)S(1)}, bf16[192,32]{0,1:T(8,128)(2,1)}, u32[]{:S(2)}) %copy-start) | copy-done | bytes 12312
  1.3 0.0 copy-start.1
  1.4 0.7 %copy-done.1 = f32[6,192]{1,0:T(8,128)S(1)} copy-done((f32[6,192]{1,0:T(8,128)S(1)}, f32[6,192]{1,0:T(8,128)}, u32[]{:S(2)}) %copy-start.1) | copy-done | bytes 4632
  2.0 0.0 copy-start.2
  2.0 0.7 %copy-done.2 = s32[192]{0:T(256)S(1)} copy-done((s32[192]{0:T(256)S(1)}, s32[192]{0:T(256)}, u32[]{:S(2)}) %copy-start.2) | copy-done | bytes 792
  2.7 0.0 copy-start.3
  2.7 0.7 %copy-done.3 = s32[192]{0:T(256)S(1)} copy-done((s32[192]{0:T(256)S(1)}, s32[192]{0:T(256)}, u32[]{:S(2)}) %copy-start.3) | copy-done | bytes 792
  3.4 16.0 %all_to_all.5.own.modes = bf16[8,64,192]{2,1,0:T(8,128)(2,1)S(1)} all-to-all(bf16[8,64,192]{2,1,0:T(8,128)(2,1)S(1)} %pack.1), channel_id=1, replica_groups={{0,2,4,6,8,10,12,14},{1,3,5,7,9,11,13,15},{16,18,20,22,24,26,28,30},{17..., dimensions={0} | all-to-all | bytes 393216 | tf_op jit(solution)/shard_map/all_to_all | solution.py:230
  19.4 0.0 collective-permute-start
  20.7 0.2 collective-permute-done.other
  20.9 8.3 %tiles.1 = (bf16[1536,1536]{1,0:T(8,128)(2,1)S(1)}, bf16[1536,1536]{1,0:T(8,128)(2,1)S(1)}, bf16[32,1536]{1,0:T(8,128)(2,1)S(1)}) custom-call(bf16[8,64,192]{2,1,0:T(8,128)(2,1)S(1)} %all_to_all.5.own.modes, bf16[8,64,192]{2,1,0:T(8,128)(2,1)S(1)} %collective-permute-done.other, f32[1]{0:T(128)S(6)} %copy.8.low_edge, f32[1]{0:T(128)S(6)} %copy.9.high_edge), custom_call_target="tpu_custom_call" | custom-call | tf_op jit(solution)/shard_map/tiles/pallas_call | solution.py:232
  29.3 0.4 collective-permute-start.1
  29.6 1.0 %collective-permute-done.1.other = bf16[32,1536]{1,0:T(8,128)(2,1)S(1)} collective-permute-done((bf16[32,1536]{1,0:T(8,128)(2,1)S(1)}, bf16[32,1536]{1,0:T(8,128)(2,1)S(1)}, u32[]{:S(2)}, u32[]{:S(2)}) %collective-permute-start.1) | collective-permute-done | bytes 98336 | tf_op jit(solution)/shard_map/ppermute | solution.py:252
  30.6 1.7 %second.1 = (f32[32,1536]{1,0:T(8,128)S(1)}, bf16[32,1536]{1,0:T(8,128)(2,1)S(1)}) custom-call(bf16[1536,1536]{1,0:T(8,128)(2,1)S(1)} %get-tuple-element.9.panel_own, bf16[1536,1536]{1,0:T(8,128)(2,1)S(1)} %get-tuple-element.10.panel_other, bf16[32,1536]{1,0:T(8,128)(2,1)S(1)} %get-tuple-element.11.own, bf16[32,1536]{1,0:T(8,128)(2,1)S(1)} %collective-permute-done.1.other, ...), custom_call_target="tpu_custom_call" | custom-call | tf_op jit(solution)/shard_map/second/pallas_call | solution.py:247
  32.4 0.4 collective-permute-start.2
  32.7 1.0 %collective-permute-done.2.other = bf16[32,1536]{1,0:T(8,128)(2,1)S(1)} collective-permute-done((bf16[32,1536]{1,0:T(8,128)(2,1)S(1)}, bf16[32,1536]{1,0:T(8,128)(2,1)S(1)}, u32[]{:S(2)}, u32[]{:S(2)}) %collective-permute-start.2) | collective-permute-done | bytes 98336 | tf_op jit(solution)/shard_map/ppermute | solution.py:254
  33.7 2.5 %image.1.sums = f32[32,128]{1,0:T(8,128)S(1)} custom-call(bf16[1536,1536]{1,0:T(8,128)(2,1)S(1)} %get-tuple-element.9.panel_own, bf16[1536,1536]{1,0:T(8,128)(2,1)S(1)} %get-tuple-element.10.panel_other, bf16[32,1536]{1,0:T(8,128)(2,1)S(1)} %get-tuple-element.12.own, bf16[32,1536]{1,0:T(8,128)(2,1)S(1)} %collective-permute-done.2.other, ...), custom_call_target="tpu_custom_call" | custom-call | tf_op jit(solution)/shard_map/image/pallas_call | solution.py:253
  36.2 0.3 collective-permute-start.3
  36.5 0.9 %collective-permute-done.3.sums_other = f32[32,128]{1,0:T(8,128)S(1)} collective-permute-done((f32[32,128]{1,0:T(8,128)S(1)}, f32[32,128]{1,0:T(8,128)S(1)}, u32[]{:S(2)}, u32[]{:S(2)}) %collective-permute-start.3) | collective-permute-done | bytes 16416 | tf_op jit(solution)/shard_map/ppermute | solution.py:261
  37.4 3.5 %ritz.1 = (f32[32,192]{1,0:T(8,128)}, f32[32,32]{1,0:T(8,128)}) custom-call(f32[32,128]{1,0:T(8,128)S(1)} %image.1.sums, f32[32,128]{1,0:T(8,128)S(1)} %collective-permute-done.3.sums_other, f32[32,1536]{1,0:T(8,128)S(1)} %get-tuple-element.13.second), custom_call_target="tpu_custom_call" | custom-call | tf_op jit(solution)/shard_map/ritz/pallas_call | solution.py:256
  (1 shorter events, 0.0 us)
Async XLA Ops:
  0.6 0.7 %copy-start = (bf16[192,32]{0,1:T(8,128)(2,1)S(1)}, bf16[192,32]{0,1:T(8,128)(2,1)}, u32[]{:S(2)}) copy-start(bf16[192,32]{0,1:T(8,128)(2,1)} %param.9) | copy-start | bytes 36868
  1.3 0.7 %copy-start.1 = (f32[6,192]{1,0:T(8,128)S(1)}, f32[6,192]{1,0:T(8,128)}, u32[]{:S(2)}) copy-start(f32[6,192]{1,0:T(8,128)} %geometry.1) | copy-start | bytes 13828
  2.0 0.7 %copy-start.2 = (s32[192]{0:T(256)S(1)}, s32[192]{0:T(256)}, u32[]{:S(2)}) copy-start(s32[192]{0:T(256)} %param.7) | copy-start | bytes 2308
  2.7 0.7 %copy-start.3 = (s32[192]{0:T(256)S(1)}, s32[192]{0:T(256)}, u32[]{:S(2)}) copy-start(s32[192]{0:T(256)} %param.8) | copy-start | bytes 2308
  19.4 1.5 %collective-permute-start = (bf16[8,64,192]{2,1,0:T(8,128)(2,1)S(1)}, bf16[8,64,192]{2,1,0:T(8,128)(2,1)S(1)}, u32[]{:S(2)}, u32[]{:S(2)}) collective-permute-start(bf16[8,64,192]{2,1,0:T(8,128)(2,1)S(1)} %all_to_all.5.own.modes), channel_id=1, source_target_pairs={{0,1},{1,0},{2,3},{3,2},{4,5},{5,4},{6,7},{7,6},{8,9},{9,8},{10,11... | collective-permute-start | bytes 589832 | tf_op jit(solution)/shard_map/ppermute | solution.py:231
  29.3 1.4 %collective-permute-start.1 = (bf16[32,1536]{1,0:T(8,128)(2,1)S(1)}, bf16[32,1536]{1,0:T(8,128)(2,1)S(1)}, u32[]{:S(2)}, u32[]{:S(2)}) collective-permute-start(bf16[32,1536]{1,0:T(8,128)(2,1)S(1)} %get-tuple-element.11.own), channel_id=1, source_target_pairs={{0,1},{1,0},{2,3},{3,2},{4,5},{5,4},{6,7},{7,6},{8,9},{9,8},{10,11... | collective-permute-start | bytes 294920 | tf_op jit(solution)/shard_map/ppermute | solution.py:252
  32.4 1.4 %collective-permute-start.2 = (bf16[32,1536]{1,0:T(8,128)(2,1)S(1)}, bf16[32,1536]{1,0:T(8,128)(2,1)S(1)}, u32[]{:S(2)}, u32[]{:S(2)}) collective-permute-start(bf16[32,1536]{1,0:T(8,128)(2,1)S(1)} %get-tuple-element.12.own), channel_id=1, source_target_pairs={{0,1},{1,0},{2,3},{3,2},{4,5},{5,4},{6,7},{7,6},{8,9},{9,8},{10,11... | collective-permute-start | bytes 294920 | tf_op jit(solution)/shard_map/ppermute | solution.py:254
  36.2 1.2 %collective-permute-start.3 = (f32[32,128]{1,0:T(8,128)S(1)}, f32[32,128]{1,0:T(8,128)S(1)}, u32[]{:S(2)}, u32[]{:S(2)}) collective-permute-start(f32[32,128]{1,0:T(8,128)S(1)} %image.1.sums), channel_id=1, source_target_pairs={{0,1},{1,0},{2,3},{3,2},{4,5},{5,4},{6,7},{7,6},{8,9},{9,8},{10,11... | collective-permute-start | bytes 49160 | tf_op jit(solution)/shard_map/ppermute | solution.py:261

commit v3 on v2

--- a/solution.py
+++ b/solution.py
@@ -16,8 +16,7 @@
 BF16 = jnp.bfloat16
 HIGHEST = lax.Precision.HIGHEST
 VMEM_SPEC = pl.BlockSpec(memory_space=pltpu.VMEM)
-SMEM_SPEC = pl.BlockSpec(memory_space=pltpu.SMEM)
-PAYLOAD_ROWS = 64
+WIDTH = 192
 TILE_ROWS = 512
 TILE_COLS = 256
 
@@ -29,28 +28,49 @@
     return high, mid, low
 
 
-def pack_body(geometry, nets, layers, modes, out):
-    shape = (1, geometry.shape[1])
+def pack_body(geometry, nets, layers, modes, out, *scratch):
+    copies = []
+    for index, source in enumerate((geometry, nets, layers, modes)):
+        copies.append(pltpu.make_async_copy(source, scratch[index], scratch[4].at[index]))
+        copies[-1].start()
+    for copy in copies:
+        copy.wait()
+    geometry, nets, layers, modes, _, sheet = scratch
     high, mid, low = pieces(geometry[...])
-    zeros = jnp.zeros((2,) + shape[1:], F32)
-    rest = jnp.zeros((8,) + shape[1:], F32)
+    zeros = jnp.zeros((2, WIDTH), F32)
     rows = jnp.concatenate(
-        [high, nets[...].astype(F32), layers[...].astype(F32), mid, zeros, low, zeros, rest], axis=0
-    ).astype(BF16)
+        [high, nets[...].astype(F32), layers[...].astype(F32), mid, zeros, low, zeros], axis=0
+    )
+    sheet[...] = jnp.zeros_like(sheet)
+    sheet[0:32, 0:WIDTH] = modes[...].astype(F32)
+    sheet[0:24, 192:256] = rows[:, 0:64]
+    sheet[32:48, 0:64] = rows[0:16, 64:128]
+    sheet[32:40, 64:128] = rows[16:24, 64:128]
+    sheet[40:48, 64:128] = rows[0:8, 128:192]
+    sheet[32:48, 128:192] = rows[8:24, 128:192]
+    packed = sheet[...].astype(BF16)
     for place in range(out.shape[0]):
-        out[place, 0:32, :] = modes[...]
-        out[place, 32:64, :] = rows
-
-
-def tile_body(scale, own, other, low_edge, high_edge, panel_own, panel_other, filtered, stage, left, right, coarse, xy, total):
-    count, _, width = own.shape
-    cols = count * width
+        out[place] = packed
+
+
+def unpack(part, stage, half):
+    for place in range(part.shape[0]):
+        start = (half * part.shape[0] + place) * WIDTH
+        sheet = part[place].astype(F32)
+        stage[0:32, start : start + WIDTH] = sheet[0:32, 0:WIDTH]
+        stage[32:56, start : start + 64] = sheet[0:24, 192:256]
+        stage[32:48, start + 64 : start + 128] = sheet[32:48, 0:64]
+        stage[48:56, start + 64 : start + 128] = sheet[32:40, 64:128]
+        stage[32:40, start + 128 : start + 192] = sheet[40:48, 64:128]
+        stage[40:56, start + 128 : start + 192] = sheet[32:48, 128:192]
+
+
+def tile_body(scale, own, other, edges, panel_own, panel_other, filtered, stage, left, right, coarse, xy, total):
+    cols = own.shape[0] * WIDTH
     rows = 2 * cols
     panels = (panel_own, panel_other)
-    for half, part in enumerate((own, other)):
-        for place in range(count):
-            start = half * cols + place * width
-            stage[:, start : start + width] = part[place].astype(F32)
+    unpack(own, stage, 0)
+    unpack(other, stage, 1)
 
     def rows_of(first, last, length):
         return stage[first:last, 0:length]
@@ -138,8 +158,7 @@
     multiply(0, last)
     generate(1, last)
     multiply(1, last)
-    centre = (low_edge[0] + high_edge[0]) * 0.5
-    half_width = (high_edge[0] - low_edge[0]) * 0.5
+    centre, half_width = edges[0:1, 0:1], edges[1:2, 0:1]
     filtered[...] = ((total[...] - centre * stage[0:32, 0:cols]) / half_width).astype(BF16)
 
 
@@ -149,15 +168,14 @@
     )
 
 
-def second_body(panel_own, panel_other, own, other, modes, low_edge, high_edge, second, second_low):
-    count, _, width = modes.shape
+def second_body(panel_own, panel_other, own, other, modes, edges, second, second_low):
+    count = modes.shape[0]
     applied = product(panel_own, panel_other, own, other)
-    centre = (low_edge[0] + high_edge[0]) * 0.5
-    half_width = (high_edge[0] - low_edge[0]) * 0.5
+    centre, half_width = edges[0:1, 0:1], edges[1:2, 0:1]
     second[...] = 2.0 * (applied - centre * own[...].astype(F32)) / half_width
     for place in range(count):
-        here = slice(place * width, place * width + width)
-        second[:, here] = second[:, here] - modes[place, 0:32, :].astype(F32)
+        here = slice(place * WIDTH, place * WIDTH + WIDTH)
+        second[:, here] = second[:, here] - modes[place, 0:32, 0:WIDTH].astype(F32)
     second_low[...] = second[...].astype(BF16)
 
 
@@ -224,18 +242,41 @@
     pair = [(i, i ^ 1) for i in range(col)]
     same_core = [[2 * chip + core for chip in range(count)] for core in range(2)]
 
-    packed = call(pack_body, "pack", shape((count, PAYLOAD_ROWS, width), BF16), [VMEM_SPEC] * 4)(
-        geometry, net_ids.reshape(1, width), layers.reshape(1, width), trial_modes.T
-    )
+    packed = call(
+        pack_body,
+        "pack",
+        shape((count, 48, 256), BF16),
+        [pl.BlockSpec(memory_space=pl.ANY)] * 4,
+        [
+            pltpu.VMEM(geometry.shape, F32),
+            pltpu.VMEM((1, width), jnp.int32),
+            pltpu.VMEM((1, width), jnp.int32),
+            pltpu.VMEM((modes, width), BF16),
+            pltpu.SemaphoreType.DMA((4,)),
+            pltpu.VMEM((48, 256), F32),
+        ],
+    )(
+        *(
+            pltpu.with_memory_space_constraint(x, pltpu.HBM)
+            for x in (
+                geometry,
+                net_ids.reshape(1, width),
+                layers.reshape(1, width),
+                trial_modes.T,
+            )
+        )
+    )
+    ends = jnp.stack([(low_edge + high_edge) * 0.5, (high_edge - low_edge) * 0.5])
+    edges = jnp.broadcast_to(ends, (2, 128))
     own = lax.all_to_all(packed, ("fil", "col"), 0, 0, axis_index_groups=same_core, tiled=True)
     other = lax.ppermute(own, "col", pair)
     panel_own, panel_other, filtered = call(
         functools.partial(tile_body, 1.0 / math.sqrt(rows)),
         "tiles",
         (pltpu.VMEM((cols, cols), BF16), pltpu.VMEM((cols, cols), BF16), shape((modes, cols), BF16)),
-        [VMEM_SPEC] * 2 + [SMEM_SPEC] * 2,
+        [VMEM_SPEC] * 3,
         [
-            pltpu.VMEM((PAYLOAD_ROWS, rows), F32),
+            pltpu.VMEM((64, rows), F32),
             pltpu.VMEM((128, rows), F32),
             pltpu.VMEM((128, cols), BF16),
             pltpu.VMEM((128, cols), BF16),
@@ -243,13 +284,13 @@
             pltpu.VMEM((modes, cols), F32),
         ],
         limit=32,
-    )(own, other, low_edge, high_edge)
+    )(own, other, edges)
     second, second_low = call(
         second_body,
         "second",
         (shape((modes, cols), F32), shape((modes, cols), BF16)),
-        [VMEM_SPEC] * 5 + [SMEM_SPEC] * 2,
-    )(panel_own, panel_other, filtered, lax.ppermute(filtered, "col", pair), own, low_edge, high_edge)
+        [VMEM_SPEC] * 6,
+    )(panel_own, panel_other, filtered, lax.ppermute(filtered, "col", pair), own, edges)
     sums = call(functools.partial(image_body, float(rows)), "image", shape((modes, 128), F32), [VMEM_SPEC] * 5)(
         panel_own, panel_other, second_low, lax.ppermute(second_low, "col", pair), second
     )
@@ -349,7 +390,7 @@
         mesh.shape["col"] % 2 == 0
         and (count // 2) % 2 == 0
         and modes == 32
-        and width % 64 == 0
+        and width == WIDTH
         and (rows // 2) % TILE_COLS == 0
         and (rows // 2) % TILE_ROWS == 0
         and rows * rows <= 16 * 1024 * 1024

time: 41.3 us -> 38.8 us (0.939)
  local copies, waits for them, and re-layouts: 2.76 us -> 0.07 us
  Pallas kernels: 16 us -> 17.2 us
  blocking collectives: 16 us -> 15 us
    unnamed x8 -> x0, local copies, waits for them, and re-layouts: 2.76 us -> none
    all_to_all x1, blocking collectives: 16 us -> 15 us  [paired_shards(): lax.all_to_all(packed, ('fil', 'col'), 0, 0, axis_index_groups=same_core,...]
    pallas_call x1, Pallas kernels: 0.02 us -> 0.9 us  [paired_shards(): call(pack_body, 'pack', shape((count, 48, 256), BF16), [pl.BlockSpec(memo...]
where the time goes in v3:
time: 38.8 us; the launch traced here: 38.4 us
  Pallas kernels  17.2 us (44%)
  blocking collectives  15 us (39%)
  waiting for transfers between devices  2.79 us (7%)
  between operations  1.96 us (5%)
  starting transfers between devices  1.31 us (3%)
    all_to_all x1, blocking collectives, paired_shards(): lax.all_to_all(packed, ('fil', 'col'), 0, 0, axis_index_groups=same_core,...  15 us
    pallas_call x1, Pallas kernels, paired_shards(): call(functools.partial(tile_body, 1.0 / math.sqrt(rows)), 'tiles', (pltpu...  8.56 us
    pallas_call x1, Pallas kernels, paired_shards(): call(functools.partial(ritz_body, ('fil', 'col', col)), 'ritz', (shape((m...  3.47 us
    pallas_call x1, Pallas kernels, paired_shards(): call(functools.partial(image_body, float(rows)), 'image', shape((modes, 1...  2.49 us
    pallas_call x1, Pallas kernels, paired_shards(): call(second_body, 'second', (shape((modes, cols), F32), shape((modes, col...  1.75 us
    ppermute x1, waiting for transfers between devices, paired_shards(): lax.ppermute(second_low, 'col', pair)  0.94 us
    ppermute x1, waiting for transfers between devices, paired_shards(): lax.ppermute(filtered, 'col', pair)  0.94 us
    pallas_call x1, Pallas kernels, paired_shards(): call(pack_body, 'pack', shape((count, 48, 256), BF16), [pl.BlockSpec(memo...  0.9 us
  transfers between devices with their start and end apart: 4, of which 4 were waited for; matrix products, arithmetic and copies ran while one was open for 0% of the time, Pallas kernels for 0%

profile of v3, /device:TPU:0, one launch (start us, length us, event | category | flops | bytes accessed | tf_op | source)
XLA Modules:
  0.0 38.4 jit_solution(13699171875450282209)
XLA Ops:
  0.6 0.9 %pack.1 = bf16[8,48,256]{2,1,0:T(8,128)(2,1)S(1)} custom-call(f32[6,192]{1,0:T(8,128)} %geometry.1, s32[1,192]{1,0:T(1,128)} %bitcast.9, s32[1,192]{1,0:T(1,128)} %bitcast.10, bf16[32,192]{1,0:T(8,128)(2,1)} %bitcast.8), custom_call_target="tpu_custom_call" | custom-call | tf_op jit(solution)/shard_map/pack/pallas_call | solution.py:245
  1.5 15.0 %all_to_all.5.own.modes = bf16[8,48,256]{2,1,0:T(8,128)(2,1)S(1)} all-to-all(bf16[8,48,256]{2,1,0:T(8,128)(2,1)S(1)} %pack.1), channel_id=1, replica_groups={{0,2,4,6,8,10,12,14},{1,3,5,7,9,11,13,15},{16,18,20,22,24,26,28,30},{17..., dimensions={0} | all-to-all | bytes 393216 | tf_op jit(solution)/shard_map/all_to_all | solution.py:271
  16.5 0.0 collective-permute-start
  17.8 0.1 maximum_bitcast_fusion
  17.9 0.1 collective-permute-done.other
  18.0 0.1 broadcast_in_dim.8.edges
  18.1 8.6 %tiles.1 = (bf16[1536,1536]{1,0:T(8,128)(2,1)S(1)}, bf16[1536,1536]{1,0:T(8,128)(2,1)S(1)}, bf16[32,1536]{1,0:T(8,128)(2,1)S(1)}) custom-call(bf16[8,48,256]{2,1,0:T(8,128)(2,1)S(1)} %all_to_all.5.own.modes, bf16[8,48,256]{2,1,0:T(8,128)(2,1)S(1)} %collective-permute-done.other, f32[2,128]{1,0:T(2,128)S(1)} %broadcast_in_dim.8.edges), custom_call_target="tpu_custom_call" | custom-call | tf_op jit(solution)/shard_map/tiles/pallas_call | solution.py:273
  26.6 0.5 %collective-permute-start.1 = (bf16[32,1536]{1,0:T(8,128)(2,1)S(1)}, bf16[32,1536]{1,0:T(8,128)(2,1)S(1)}, u32[]{:S(2)}, u32[]{:S(2)}) collective-permute-start(bf16[32,1536]{1,0:T(8,128)(2,1)S(1)} %get-tuple-element.11.own), channel_id=1, source_target_pairs={{0,1},{1,0},{2,3},{3,2},{4,5},{5,4},{6,7},{7,6},{8,9},{9,8},{10,11... | collective-permute-start | bytes 294920 | tf_op jit(solution)/shard_map/ppermute | solution.py:293
  27.1 0.9 %collective-permute-done.1.other = bf16[32,1536]{1,0:T(8,128)(2,1)S(1)} collective-permute-done((bf16[32,1536]{1,0:T(8,128)(2,1)S(1)}, bf16[32,1536]{1,0:T(8,128)(2,1)S(1)}, u32[]{:S(2)}, u32[]{:S(2)}) %collective-permute-start.1) | collective-permute-done | bytes 98336 | tf_op jit(solution)/shard_map/ppermute | solution.py:293
  28.1 1.7 %second.1 = (f32[32,1536]{1,0:T(8,128)S(1)}, bf16[32,1536]{1,0:T(8,128)(2,1)S(1)}) custom-call(bf16[1536,1536]{1,0:T(8,128)(2,1)S(1)} %get-tuple-element.9.panel_own, bf16[1536,1536]{1,0:T(8,128)(2,1)S(1)} %get-tuple-element.10.panel_other, bf16[32,1536]{1,0:T(8,128)(2,1)S(1)} %get-tuple-element.11.own, bf16[32,1536]{1,0:T(8,128)(2,1)S(1)} %collective-permute-done.1.other, ...), custom_call_target="tpu_custom_call" | custom-call | tf_op jit(solution)/shard_map/second/pallas_call | solution.py:288
  29.8 0.4 %collective-permute-start.2 = (bf16[32,1536]{1,0:T(8,128)(2,1)S(1)}, bf16[32,1536]{1,0:T(8,128)(2,1)S(1)}, u32[]{:S(2)}, u32[]{:S(2)}) collective-permute-start(bf16[32,1536]{1,0:T(8,128)(2,1)S(1)} %get-tuple-element.12.own), channel_id=1, source_target_pairs={{0,1},{1,0},{2,3},{3,2},{4,5},{5,4},{6,7},{7,6},{8,9},{9,8},{10,11... | collective-permute-start | bytes 294920 | tf_op jit(solution)/shard_map/ppermute | solution.py:295
  30.2 0.9 %collective-permute-done.2.other = bf16[32,1536]{1,0:T(8,128)(2,1)S(1)} collective-permute-done((bf16[32,1536]{1,0:T(8,128)(2,1)S(1)}, bf16[32,1536]{1,0:T(8,128)(2,1)S(1)}, u32[]{:S(2)}, u32[]{:S(2)}) %collective-permute-start.2) | collective-permute-done | bytes 98336 | tf_op jit(solution)/shard_map/ppermute | solution.py:295
  31.2 2.5 %image.1.sums = f32[32,128]{1,0:T(8,128)S(1)} custom-call(bf16[1536,1536]{1,0:T(8,128)(2,1)S(1)} %get-tuple-element.9.panel_own, bf16[1536,1536]{1,0:T(8,128)(2,1)S(1)} %get-tuple-element.10.panel_other, bf16[32,1536]{1,0:T(8,128)(2,1)S(1)} %get-tuple-element.12.own, bf16[32,1536]{1,0:T(8,128)(2,1)S(1)} %collective-permute-done.2.other, ...), custom_call_target="tpu_custom_call" | custom-call | tf_op jit(solution)/shard_map/image/pallas_call | solution.py:294
  33.7 0.4 collective-permute-start.3
  34.1 0.8 %collective-permute-done.3.sums_other = f32[32,128]{1,0:T(8,128)S(1)} collective-permute-done((f32[32,128]{1,0:T(8,128)S(1)}, f32[32,128]{1,0:T(8,128)S(1)}, u32[]{:S(2)}, u32[]{:S(2)}) %collective-permute-start.3) | collective-permute-done | bytes 16416 | tf_op jit(solution)/shard_map/ppermute | solution.py:302
  34.9 3.5 %ritz.1 = (f32[32,192]{1,0:T(8,128)}, f32[32,32]{1,0:T(8,128)}) custom-call(f32[32,128]{1,0:T(8,128)S(1)} %image.1.sums, f32[32,128]{1,0:T(8,128)S(1)} %collective-permute-done.3.sums_other, f32[32,1536]{1,0:T(8,128)S(1)} %get-tuple-element.13.second), custom_call_target="tpu_custom_call" | custom-call | tf_op jit(solution)/shard_map/ritz/pallas_call | solution.py:297
Async XLA Ops:
  16.5 1.4 %collective-permute-start = (bf16[8,48,256]{2,1,0:T(8,128)(2,1)S(1)}, bf16[8,48,256]{2,1,0:T(8,128)(2,1)S(1)}, u32[]{:S(2)}, u32[]{:S(2)}) collective-permute-start(bf16[8,48,256]{2,1,0:T(8,128)(2,1)S(1)} %all_to_all.5.own.modes), channel_id=1, source_target_pairs={{0,1},{1,0},{2,3},{3,2},{4,5},{5,4},{6,7},{7,6},{8,9},{9,8},{10,11... | collective-permute-start | bytes 589832 | tf_op jit(solution)/shard_map/ppermute | solution.py:272
  26.6 1.5 %collective-permute-start.1 = (bf16[32,1536]{1,0:T(8,128)(2,1)S(1)}, bf16[32,1536]{1,0:T(8,128)(2,1)S(1)}, u32[]{:S(2)}, u32[]{:S(2)}) collective-permute-start(bf16[32,1536]{1,0:T(8,128)(2,1)S(1)} %get-tuple-element.11.own), channel_id=1, source_target_pairs={{0,1},{1,0},{2,3},{3,2},{4,5},{5,4},{6,7},{7,6},{8,9},{9,8},{10,11... | collective-permute-start | bytes 294920 | tf_op jit(solution)/shard_map/ppermute | solution.py:293
  29.8 1.4 %collective-permute-start.2 = (bf16[32,1536]{1,0:T(8,128)(2,1)S(1)}, bf16[32,1536]{1,0:T(8,128)(2,1)S(1)}, u32[]{:S(2)}, u32[]{:S(2)}) collective-permute-start(bf16[32,1536]{1,0:T(8,128)(2,1)S(1)} %get-tuple-element.12.own), channel_id=1, source_target_pairs={{0,1},{1,0},{2,3},{3,2},{4,5},{5,4},{6,7},{7,6},{8,9},{9,8},{10,11... | collective-permute-start | bytes 294920 | tf_op jit(solution)/shard_map/ppermute | solution.py:295
  33.7 1.2 %collective-permute-start.3 = (f32[32,128]{1,0:T(8,128)S(1)}, f32[32,128]{1,0:T(8,128)S(1)}, u32[]{:S(2)}, u32[]{:S(2)}) collective-permute-start(f32[32,128]{1,0:T(8,128)S(1)} %image.1.sums), channel_id=1, source_target_pairs={{0,1},{1,0},{2,3},{3,2},{4,5},{5,4},{6,7},{7,6},{8,9},{9,8},{10,11... | collective-permute-start | bytes 49160 | tf_op jit(solution)/shard_map/ppermute | solution.py:302

commit v4 on v3

v4 whole, which is shorter than its diff:
```python
import functools
import math

import jax
import jax.numpy as jnp
from jax import lax
from jax.experimental import pallas as pl
from jax.experimental.pallas import tpu as pltpu
from jax.sharding import PartitionSpec as P

SHIELD_FACTOR = 0.5
LAYER_PITCH = 0.02
NETS = 4
LAYERS = 8
F32 = jnp.float32
BF16 = jnp.bfloat16
HIGHEST = lax.Precision.HIGHEST
VMEM_SPEC = pl.BlockSpec(memory_space=pltpu.VMEM)
WIDTH = 192
TILE_ROWS = 512
TILE_COLS = 256


def pieces(x):
    high = x.astype(BF16).astype(F32)
    mid = (x - high).astype(BF16).astype(F32)
    low = (x - high - mid).astype(BF16).astype(F32)
    return high, mid, low


def pack_body(geometry, nets, layers, modes, out, *scratch):
    copies = []
    for index, source in enumerate((geometry, nets, layers, modes)):
        copies.append(pltpu.make_async_copy(source, scratch[index], scratch[4].at[index]))
        copies[-1].start()
    for copy in copies:
        copy.wait()
    geometry, nets, layers, modes, _, sheet = scratch
    high, mid, low = pieces(geometry[...])
    zeros = jnp.zeros((2, WIDTH), F32)
    rows = jnp.concatenate(
        [high, nets[...].astype(F32), layers[...].astype(F32), mid, zeros, low, zeros], axis=0
    )
    sheet[...] = jnp.zeros_like(sheet)
    sheet[0:32, 0:WIDTH] = modes[...].astype(F32)
    sheet[0:24, 192:256] = rows[:, 0:64]
    sheet[32:48, 0:64] = rows[0:16, 64:128]
    sheet[32:40, 64:128] = rows[16:24, 64:128]
    sheet[40:48, 64:128] = rows[0:8, 128:192]
    sheet[32:48, 128:192] = rows[8:24, 128:192]
    packed = sheet[...].astype(BF16)
    for place in range(out.shape[0]):
        out[place] = packed


def unpack(part, stage):
    for place in range(part.shape[0]):
        start = place * WIDTH
        sheet = part[place].astype(F32)
        stage[0:32, start : start + WIDTH] = sheet[0:32, 0:WIDTH]
        stage[32:56, start : start + 64] = sheet[0:24, 192:256]
        stage[32:48, start + 64 : start + 128] = sheet[32:48, 0:64]
        stage[48:56, start + 64 : start + 128] = sheet[32:40, 64:128]
        stage[32:40, start + 128 : start + 192] = sheet[40:48, 64:128]
        stage[40:56, start + 128 : start + 192] = sheet[32:48, 128:192]


def net_groups(base, nets):
    listed = [base] + [jnp.where(nets == float(n), base, 0.0) for n in range(NETS)]
    return jnp.concatenate(listed, axis=0)


def left_operand(stage, left):
    length = stage.shape[1]
    nets = stage[38:39, :]
    segment = [net_groups(stage[s + 2 : s + 5, :], nets) for s in (32, 40, 48)]
    place_x = [stage[s : s + 1, :] for s in (32, 40, 48)]
    place_y = [stage[s + 1 : s + 2, :] for s in (32, 40, 48)]
    spare = place_x + place_y
    for index, piece in enumerate((0, 0, 1, 1, 0, 2)):
        left[16 * index : 16 * index + 16, :] = jnp.concatenate([segment[piece], spare[index]], axis=0)
    levels = lax.broadcasted_iota(jnp.int32, (LAYERS, length), 0).astype(F32)
    chosen = jnp.where(levels == stage[39:40, :], 1.0, 0.0)
    left[96:104, :] = chosen
    left[104:112, :] = chosen
    left[112:120, :] = chosen
    ones = jnp.ones((3, length), F32)
    left[120:128, :] = jnp.concatenate([*squares(stage), ones, jnp.zeros((2, length), F32)], axis=0)


def squares(stage):
    return pieces(jnp.square(stage[37:38, :] + stage[45:46, :] + stage[53:54, :]))


def right_operand(scale, stage, right, coarse, places):
    cols = stage.shape[1]
    nets = stage[38:39, :]
    base = (stage[34:37, :] + stage[42:45, :] + stage[50:53, :]) * (SHIELD_FACTOR * scale)
    scaled = [net_groups(piece, nets) for piece in pieces(base)]
    blank = jnp.zeros((1, cols), F32)
    for index, piece in enumerate((0, 1, 0, 1, 2, 0)):
        right[16 * index : 16 * index + 16, :] = jnp.concatenate([scaled[piece], blank], axis=0).astype(BF16)
    right[96:128, :] = jnp.zeros((32, cols), BF16)
    coarse[0:96, :] = jnp.zeros((96, cols), BF16)
    levels = lax.broadcasted_iota(jnp.int32, (LAYERS, cols), 0).astype(F32)
    gap = levels * LAYER_PITCH - stage[39:40, :] * LAYER_PITCH
    ones = jnp.ones((3, cols), F32)
    coarse[96:128, :] = jnp.concatenate(
        [*pieces(gap * gap), ones, *squares(stage), jnp.zeros((2, cols), F32)], axis=0
    ).astype(BF16)
    places[...] = stage[32:40, :] + stage[40:48, :] + stage[48:56, :]


def place_columns():
    line = lax.broadcasted_iota(jnp.int32, (128, 256), 0)
    lane = lax.broadcasted_iota(jnp.int32, (128, 256), 1)
    for_x = (lane < 128) & ((line == 15) | (line == 31) | (line == 47))
    for_y = (lane >= 128) & ((line == 63) | (line == 79) | (line == 95))
    return jnp.where(for_x | for_y, 1.0, 0.0).astype(BF16)


def generate(left, right, coarse, places, panel, start):
    here = slice(start, start + TILE_ROWS)
    feats = left[:, here].T.astype(BF16)
    tall = jnp.dot(feats, place_columns(), preferred_element_type=F32)
    tall_x = jnp.concatenate([tall[:, 0:128]] * (TILE_COLS // 128), axis=1)
    tall_y = jnp.concatenate([tall[:, 128:256]] * (TILE_COLS // 128), axis=1)
    for first in range(0, panel.shape[1], TILE_COLS):
        there = slice(first, first + TILE_COLS)
        aligned = jnp.dot(feats, right[:, there], preferred_element_type=F32)
        spread = jnp.dot(feats, coarse[:, there], preferred_element_type=F32)
        delta_x = tall_x - places[0:1, there]
        delta_y = tall_y - places[1:2, there]
        spread = delta_x * delta_x + delta_y * delta_y + spread
        panel[here, there] = (aligned * lax.rsqrt(spread)).astype(BF16)


def partial_product(modes, panel, start):
    here = slice(start, start + TILE_ROWS)
    return jnp.dot(modes[:, here], panel[here, :], preferred_element_type=F32)


def own_tiles_body(scale, own, panel, right, coarse, places, modes, total, stage, left):
    unpack(own, stage)
    left_operand(stage, left)
    right_operand(scale, stage, right, coarse, places)
    modes[...] = stage[0:32, :].astype(BF16)
    cols = panel.shape[0]
    generate(left, right, coarse, places, panel, 0)
    for start in range(TILE_ROWS, cols, TILE_ROWS):
        done = partial_product(modes, panel, start - TILE_ROWS)
        total[...] = done if start == TILE_ROWS else total[...] + done
        generate(left, right, coarse, places, panel, start)
    total[...] += partial_product(modes, panel, cols - TILE_ROWS)


def other_tiles_body(other, right, coarse, places, modes, total, low_edge, high_edge, panel, filtered, stage, left, others):
    unpack(other, stage)
    left_operand(stage, left)
    others[...] = stage[0:32, :].astype(BF16)
    cols = panel.shape[0]
    applied = total[...]
    generate(left, right, coarse, places, panel, 0)
    for start in range(TILE_ROWS, cols, TILE_ROWS):
        applied = applied + partial_product(others, panel, start - TILE_ROWS)
        generate(left, right, coarse, places, panel, start)
    applied = applied + partial_product(others, panel, cols - TILE_ROWS)
    centre = (low_edge[...] + high_edge[...]) * 0.5
    half_width = (high_edge[...] - low_edge[...]) * 0.5
    filtered[...] = ((applied - centre * modes[...].astype(F32)) / half_width).astype(BF16)


def half_body(panel, own, part):
    part[...] = jnp.dot(own[...], panel[...], preferred_element_type=F32)


def second_body(panel, other, part, own, modes, low_edge, high_edge, second, second_low):
    applied = part[...] + jnp.dot(other[...], panel[...], preferred_element_type=F32)
    centre = (low_edge[...] + high_edge[...]) * 0.5
    half_width = (high_edge[...] - low_edge[...]) * 0.5
    value = 2.0 * (applied - centre * own[...].astype(F32)) / half_width - modes[...].astype(F32)
    second[...] = value
    second_low[...] = value.astype(BF16)


def outer(a, b):
    return lax.dot_general(a, b, (((1,), (1,)), ((), ())), precision=HIGHEST, preferred_element_type=F32)


def gram_body(filaments, second, gram):
    gram[...] = outer(second[...], second[...]) / filaments


def image_body(filaments, panel, other, part, second, gram, gram_other, cross, inverse):
    modes = gram.shape[0]
    line = lax.broadcasted_iota(jnp.int32, (modes, modes), 0)
    lane = lax.broadcasted_iota(jnp.int32, (modes, modes), 1)
    unit = jnp.where(lane == line, 1.0, 0.0)
    system = jnp.concatenate([gram[...] + gram_other[...], unit], axis=1)
    applied = part[...] + jnp.dot(other[...], panel[...], preferred_element_type=F32)
    cross[...] = outer(second[...], applied) / filaments
    for pivot in range(modes):
        row = system[pivot : pivot + 1, :]
        column = system[:, pivot : pivot + 1] / system[pivot : pivot + 1, pivot : pivot + 1]
        column = jnp.where(line[:, 0:1] > pivot, column, 0.0)
        system = system - column * row
    diagonal = jnp.sum(system[:, 0:modes] * unit, axis=1, keepdims=True)
    inverse[...] = system[:, modes : 2 * modes] / jnp.sqrt(diagonal)


def ritz_body(axes, inverse, second, ritz):
    width = ritz.shape[1]
    fil, col, col_size = axes
    place = lax.axis_index(fil) * (col_size // 2) + lax.axis_index(col) // 2
    odd = place % 2
    start = (place // 2) * (2 * width) + odd * (width - 64)
    window = second[:, pl.ds(pl.multiple_of(start, 128), width + 64)]
    moved = pltpu.roll(window, width, 1)
    mine = jnp.where(odd == 1, moved, window)[:, 0:width]
    ritz[...] = jnp.dot(inverse[...], mine, precision=HIGHEST, preferred_element_type=F32)


def projected_body(inverse, cross, cross_other, projected):
    half_solved = jnp.dot(
        inverse[...], cross[...] + cross_other[...], precision=HIGHEST, preferred_element_type=F32
    )
    projected[...] = outer(half_solved, inverse[...])


def call(body, name, out_shape, in_specs, scratch=(), limit=16, work=0):
    return pl.pallas_call(
        body,
        name=name,
        out_shape=out_shape,
        in_specs=in_specs,
        out_specs=jax.tree.map(lambda _: VMEM_SPEC, out_shape),
        scratch_shapes=list(scratch),
        compiler_params=pltpu.CompilerParams(vmem_limit_bytes=limit * 1024 * 1024),
        cost_estimate=pl.CostEstimate(flops=2 * work, bytes_accessed=0, transcendentals=0) if work else None,
    )


def paired_shards(geometry, net_ids, layers, trial_modes, low_edge, high_edge):
    width, modes = trial_modes.shape
    fil, col = lax.axis_size("fil"), lax.axis_size("col")
    count = fil * col // 2
    cols = count * width
    rows = 2 * cols
    shape = jax.ShapeDtypeStruct
    pair = [(i, i ^ 1) for i in range(col)]
    same_core = [[2 * chip + core for chip in range(count)] for core in range(2)]

    packed = call(
        pack_body,
        "pack",
        shape((count, 48, 256), BF16),
        [pl.BlockSpec(memory_space=pl.ANY)] * 4,
        [
            pltpu.VMEM(geometry.shape, F32),
            pltpu.VMEM((1, width), jnp.int32),
            pltpu.VMEM((1, width), jnp.int32),
            pltpu.VMEM((modes, width), BF16),
            pltpu.SemaphoreType.DMA((4,)),
            pltpu.VMEM((48, 256), F32),
        ],
    )(
        *(
            pltpu.with_memory_space_constraint(x, pltpu.HBM)
            for x in (
                geometry,
                net_ids.reshape(1, width),
                layers.reshape(1, width),
                trial_modes.T,
            )
        )
    )
    edges = (low_edge.reshape(1, 1), high_edge.reshape(1, 1))
    own = lax.all_to_all(packed, ("fil", "col"), 0, 0, axis_index_groups=same_core, tiled=True)
    other = lax.ppermute(own, "col", pair)
    square = pltpu.VMEM((cols, cols), BF16)
    operand = shape((128, cols), BF16)
    stages = [pltpu.VMEM((64, cols), F32), pltpu.VMEM((128, cols), F32)]
    panel_own, right, coarse, places, low, total = call(
        functools.partial(own_tiles_body, 1.0 / math.sqrt(rows)),
        "own_tiles",
        (square, operand, operand, shape((8, cols), F32), shape((modes, cols), BF16), shape((modes, cols), F32)),
        [VMEM_SPEC],
        stages,
        work=cols * cols * 160,
    )(own)
    panel_other, filtered = call(
        other_tiles_body,
        "other_tiles",
        (square, shape((modes, cols), BF16)),
        [VMEM_SPEC] * 8,
        [*stages, pltpu.VMEM((modes, cols), BF16)],
        work=cols * cols * 160,
    )(other, right, coarse, places, low, total, *edges)

    half = call(half_body, "half", shape((modes, cols), F32), [VMEM_SPEC] * 2, work=cols * cols * modes)
    filtered_other = lax.ppermute(filtered, "col", pair)
    second, second_low = call(
        second_body,
        "second",
        (shape((modes, cols), F32), shape((modes, cols), BF16)),
        [VMEM_SPEC] * 7,
    )(panel_other, filtered_other, half(panel_own, filtered), filtered, low, *edges)
    second_other = lax.ppermute(second_low, "col", pair)
    gram = call(functools.partial(gram_body, float(rows)), "gram", shape((modes, modes), F32), [VMEM_SPEC])(second)
    gram_other = lax.ppermute(gram, "col", pair)
    cross, inverse = call(
        functools.partial(image_body, float(rows)),
        "image",
        (shape((modes, modes), F32), shape((modes, modes), F32)),
        [VMEM_SPEC] * 6,
    )(panel_other, second_other, half(panel_own, second_low), second, gram, gram_other)
    cross_other = lax.ppermute(cross, "col", pair)
    ritz = call(
        functools.partial(ritz_body, ("fil", "col", col)), "ritz", shape((modes, width), F32), [VMEM_SPEC] * 2
    )(inverse, second)
    projected = call(projected_body, "projected", shape((modes, modes), F32), [VMEM_SPEC] * 3)(
        inverse, cross, cross_other
    )
    return ritz.T, projected


def features(geometry, net_ids, layers):
    height = layers.astype(F32) * LAYER_PITCH
    return jnp.concatenate([geometry[0:2], height[None], geometry[2:6], net_ids.astype(F32)[None]], axis=0)


def kernel_tile(row_feat, col_feat, kernel_scale):
    delta_x = row_feat[0][:, None] - col_feat[0][None, :]
    delta_y = row_feat[1][:, None] - col_feat[1][None, :]
    delta_z = row_feat[2][:, None] - col_feat[2][None, :]
    radius_sq = (
        row_feat[6][:, None] * row_feat[6][:, None] + col_feat[6][None, :] * col_feat[6][None, :]
    )
    spread = delta_x * delta_x + delta_y * delta_y + delta_z * delta_z + radius_sq
    alignment = (
        row_feat[3][:, None] * col_feat[3][None, :]
        + row_feat[4][:, None] * col_feat[4][None, :]
        + row_feat[5][:, None] * col_feat[5][None, :]
    )
    couple = jnp.where(row_feat[7][:, None] == col_feat[7][None, :], 1.0, SHIELD_FACTOR)
    return (alignment * couple * lax.rsqrt(spread) * kernel_scale).astype(BF16)


def column_span(length, tile_rows, shard_rows):
    span_limit = max(shard_rows, (1 << 20) // tile_rows)
    span_cols = shard_rows
    while span_cols * 2 <= span_limit and length % (span_cols * 2) == 0:
        span_cols = span_cols * 2
    return span_cols


def accumulate(running, row_feat, part_feats, gathered, kernel_scale, span_cols):
    turns = gathered.shape[0] // span_cols

    def one_span(turn_index, partial_sum):
        offset = turn_index * span_cols
        span_feats = lax.dynamic_slice_in_dim(part_feats, offset, span_cols, 1)
        span_modes = lax.dynamic_slice_in_dim(gathered, offset, span_cols, 0)
        tile_vals = kernel_tile(row_feat, span_feats, kernel_scale)
        return partial_sum + jnp.dot(tile_vals, span_modes, preferred_element_type=F32)

    return lax.fori_loop(0, turns, one_span, running)


def general_shards(geometry, net_ids, layers, trial_modes, low_edge, high_edge):
    own_rows, modes_count = trial_modes.shape
    filaments = own_rows * lax.axis_size("fil") * lax.axis_size("col")
    kernel_scale = 1.0 / math.sqrt(filaments)
    own_feats = features(geometry, net_ids, layers)
    row_feat = lax.all_gather(own_feats, "col", axis=1, tiled=True)
    col_feat = lax.all_gather(own_feats, "fil", axis=1, tiled=True)
    tile_rows = row_feat.shape[1]

    def apply_operator(mode_block):
        gathered = lax.all_gather(mode_block, "fil", axis=0, tiled=True)
        initial = jnp.zeros((tile_rows, modes_count), F32)
        span = column_span(gathered.shape[0], tile_rows, own_rows)
        partial_value = accumulate(initial, row_feat, col_feat, gathered, kernel_scale, span)
        summed = lax.psum(partial_value, "col")
        return lax.dynamic_slice_in_dim(summed, lax.axis_index("col") * own_rows, own_rows, 0)

    centre = (low_edge[0] + high_edge[0]) * 0.5
    half_width = (high_edge[0] - low_edge[0]) * 0.5
    filtered_one = (
        (apply_operator(trial_modes) - centre * trial_modes.astype(F32)) / half_width
    ).astype(BF16)
    second = 2.0 * (
        apply_operator(filtered_one) - centre * filtered_one.astype(F32)
    ) / half_width - trial_modes.astype(F32)
    second_low = second.astype(BF16)
    gram_local = jnp.dot(second.T, second, precision=HIGHEST) / filaments
    image_block = apply_operator(second_low)
    cross_local = jnp.dot(second.T, image_block, precision=HIGHEST) / filaments
    gram_matrix, cross_matrix = lax.psum((gram_local, cross_local), ("fil", "col"))
    factor = jnp.linalg.cholesky(gram_matrix)
    ritz_basis = jax.scipy.linalg.solve_triangular(factor, second.T, lower=True).T
    half_solved = jax.scipy.linalg.solve_triangular(factor, cross_matrix, lower=True)
    projected = jax.scipy.linalg.solve_triangular(factor, half_solved.T, lower=True).T
    return (ritz_basis, projected)


def fits(mesh, width, modes):
    count = mesh.shape["fil"] * mesh.shape["col"]
    rows = count * width
    return (
        mesh.shape["col"] % 2 == 0
        and (count // 2) % 2 == 0
        and modes == 32
        and width == WIDTH
        and (rows // 2) % TILE_COLS == 0
        and (rows // 2) % TILE_ROWS == 0
        and rows * rows <= 16 * 1024 * 1024
    )


def solution(mesh):
    in_specs = (
        P(None, ("groups", "fil", "col")),
        P(("groups", "fil", "col")),
        P(("groups", "fil", "col")),
        P(("groups", "fil", "col"), None),
        P("groups"),
        P("groups"),
    )
    out_specs = (P(("groups", "fil", "col"), None), P("groups", None))

    def shards(geometry, net_ids, layers, trial_modes, low_edge, high_edge):
        form = paired_shards if fits(mesh, *trial_modes.shape) else general_shards
        return form(geometry, net_ids, layers, trial_modes, low_edge, high_edge)

    return jax.shard_map(shards, mesh=mesh, in_specs=in_specs, out_specs=out_specs, check_vma=False)
```

time: 38.8 us -> 35.1 us (0.905)
  waiting for transfers between devices: 2.79 us -> 0.28 us
  Pallas kernels: 17.2 us -> 16.1 us
    ppermute x3 -> x4, waiting for transfers between devices: 2.73 us -> 0.28 us  [the longest x1 0.13 us: paired_shards(): gram_other = lax.ppermute(gram, 'col', pair)]
    pallas_call x1, Pallas kernels: 1.75 us -> 0.92 us  [paired_shards(): call(second_body, 'second', (shape((modes, cols), F32), shape((modes, col...]
    pallas_call x3 -> x8, Pallas kernels: 14.5 us -> 14.3 us  [the longest x1 3.84 us: paired_shards(): call(functools.partial(own_tiles_body, 1.0 / math.sqrt(rows)), 'own_tiles...]
    ppermute x3 -> x4, starting transfers between devices: 1.31 us -> 1.41 us  [the longest x1 0.57 us: paired_shards(): filtered_other = lax.ppermute(filtered, 'col', pair)]
  transfers between devices with their start and end apart: 4 -> 5, of which waited for: 4 -> 2; matrix products, arithmetic and copies ran while one was open for 0% -> 0% of each run, Pallas kernels for 0% -> 20%
where the time goes in v4:
time: 35.1 us; the launch traced here: 34.7 us
  Pallas kernels  16.1 us (46%)
  blocking collectives  15 us (43%)
  between operations  1.96 us (6%)
  starting transfers between devices  1.41 us (4%)
    all_to_all x1, blocking collectives, paired_shards(): lax.all_to_all(packed, ('fil', 'col'), 0, 0, axis_index_groups=same_core,...  15 us
    pallas_call x1, Pallas kernels, paired_shards(): call(functools.partial(own_tiles_body, 1.0 / math.sqrt(rows)), 'own_tiles...  3.84 us
    pallas_call x1, Pallas kernels, paired_shards(): call(other_tiles_body, 'other_tiles', (square, shape((modes, cols), BF16)...  3.8 us
    pallas_call x1, Pallas kernels, paired_shards(): call(functools.partial(image_body, float(rows)), 'image', (shape((modes,...  2.78 us
    pallas_call x1, Pallas kernels, paired_shards(): call(second_body, 'second', (shape((modes, cols), F32), shape((modes, col...  0.92 us
    pallas_call x1, Pallas kernels, paired_shards(): call(projected_body, 'projected', shape((modes, modes), F32), [VMEM_SPEC]...  0.91 us
    pallas_call x1, Pallas kernels, paired_shards(): call(pack_body, 'pack', shape((count, 48, 256), BF16), [pl.BlockSpec(memo...  0.9 us
    pallas_call x1, Pallas kernels, paired_shards(): half(panel_own, filtered)  0.89 us
  transfers between devices with their start and end apart: 5, of which 2 were waited for; matrix products, arithmetic and copies ran while one was open for 0% of the time, Pallas kernels for 20%

profile of v4, /device:TPU:0, one launch (start us, length us, event | category | flops | bytes accessed | tf_op | source)
XLA Modules:
  0.0 34.7 jit_solution(10459661469544043699)
XLA Ops:
  0.6 0.9 %pack.1 = bf16[8,48,256]{2,1,0:T(8,128)(2,1)S(1)} custom-call(f32[6,192]{1,0:T(8,128)} %geometry.1, s32[1,192]{1,0:T(1,128)} %bitcast.12, s32[1,192]{1,0:T(1,128)} %bitcast.13, bf16[32,192]{1,0:T(8,128)(2,1)} %bitcast.11), custom_call_target="tpu_custom_call" | custom-call | tf_op jit(solution)/shard_map/pack/pallas_call | solution.py:253
  1.5 15.0 %all_to_all.5.own = bf16[8,48,256]{2,1,0:T(8,128)(2,1)S(1)} all-to-all(bf16[8,48,256]{2,1,0:T(8,128)(2,1)S(1)} %pack.1), channel_id=1, replica_groups={{0,2,4,6,8,10,12,14},{1,3,5,7,9,11,13,15},{16,18,20,22,24,26,28,30},{17..., dimensions={0} | all-to-all | bytes 393216 | tf_op jit(solution)/shard_map/all_to_all | solution.py:278
  16.5 0.0 collective-permute-start
  17.8 3.8 %own_tiles.1 = (bf16[1536,1536]{1,0:T(8,128)(2,1)S(1)}, bf16[128,1536]{1,0:T(8,128)(2,1)S(1)}, bf16[128,1536]{1,0:T(8,128)(2,1)S(1)}, f32[8,1536]{1,0:T(8,128)S(...) custom-call(bf16[8,48,256]{2,1,0:T(8,128)(2,1)S(1)} %all_to_all.5.own), custom_call_target="tpu_custom_call" | custom-call | flops 754974720 | tf_op jit(solution)/shard_map/own_tiles/pallas_call | solution.py:283
  21.7 0.0 collective-permute-done.other
  21.7 3.8 %other_tiles.1 = (bf16[1536,1536]{1,0:T(8,128)(2,1)S(1)}, bf16[32,1536]{1,0:T(8,128)(2,1)S(1)}) custom-call(bf16[8,48,256]{2,1,0:T(8,128)(2,1)S(1)} %collective-permute-done.other, bf16[128,1536]{1,0:T(8,128)(2,1)S(1)} %get-tuple-element.14.right, bf16[128,1536]{1,0:T(8,128)(2,1)S(1)} %get-tuple-element.15.coarse, f32[8,1536]{1,0:T(8,128)S(1)} %get-tuple-element.16.places, ...), custom_call_target="tpu_custom_call" | custom-call | flops 754974720 | tf_op jit(solution)/shard_map/other_tiles/pallas_call | solution.py:291
  25.5 0.6 %collective-permute-start.1 = (bf16[32,1536]{1,0:T(8,128)(2,1)S(1)}, bf16[32,1536]{1,0:T(8,128)(2,1)S(1)}, u32[]{:S(2)}, u32[]{:S(2)}) collective-permute-start(bf16[32,1536]{1,0:T(8,128)(2,1)S(1)} %get-tuple-element.20.own), channel_id=1, source_target_pairs={{0,1},{1,0},{2,3},{3,2},{4,5},{5,4},{6,7},{7,6},{8,9},{9,8},{10,11... | collective-permute-start | bytes 294920 | tf_op jit(solution)/shard_map/ppermute | solution.py:301
  26.1 0.9 %half.2.part = f32[32,1536]{1,0:T(8,128)S(1)} custom-call(bf16[1536,1536]{1,0:T(8,128)(2,1)S(1)} %get-tuple-element.21.panel, bf16[32,1536]{1,0:T(8,128)(2,1)S(1)} %get-tuple-element.20.own), custom_call_target="tpu_custom_call" | custom-call | flops 150994944 | tf_op jit(solution)/shard_map/half/pallas_call | solution.py:307
  27.0 0.0 collective-permute-done.1.other
  27.0 0.9 %second.1 = (f32[32,1536]{1,0:T(8,128)S(1)}, bf16[32,1536]{1,0:T(8,128)(2,1)S(1)}) custom-call(bf16[1536,1536]{1,0:T(8,128)(2,1)S(1)} %get-tuple-element.19.panel, bf16[32,1536]{1,0:T(8,128)(2,1)S(1)} %collective-permute-done.1.other, f32[32,1536]{1,0:T(8,128)S(1)} %half.2.part, bf16[32,1536]{1,0:T(8,128)(2,1)S(1)} %get-tuple-element.20.own, ...), custom_call_target="tpu_custom_call" | custom-call | tf_op jit(solution)/shard_map/second/pallas_call | solution.py:302
  27.9 0.4 %collective-permute-start.2 = (bf16[32,1536]{1,0:T(8,128)(2,1)S(1)}, bf16[32,1536]{1,0:T(8,128)(2,1)S(1)}, u32[]{:S(2)}, u32[]{:S(2)}) collective-permute-start(bf16[32,1536]{1,0:T(8,128)(2,1)S(1)} %get-tuple-element.22.own), channel_id=1, source_target_pairs={{0,1},{1,0},{2,3},{3,2},{4,5},{5,4},{6,7},{7,6},{8,9},{9,8},{10,11... | collective-permute-start | bytes 294920 | tf_op jit(solution)/shard_map/ppermute | solution.py:308
  28.4 0.3 gram.1
  28.7 0.2 collective-permute-start.3
  28.8 0.9 %half.3.part = f32[32,1536]{1,0:T(8,128)S(1)} custom-call(bf16[1536,1536]{1,0:T(8,128)(2,1)S(1)} %get-tuple-element.21.panel, bf16[32,1536]{1,0:T(8,128)(2,1)S(1)} %get-tuple-element.22.own), custom_call_target="tpu_custom_call" | custom-call | flops 150994944 | tf_op jit(solution)/shard_map/half/pallas_call | solution.py:316
  29.7 0.1 collective-permute-done.3.gram_other
  29.8 0.0 collective-permute-done.2.other
  29.9 2.8 %image.1 = (f32[32,32]{1,0:T(8,128)S(1)}, f32[32,32]{1,0:T(8,128)S(1)}) custom-call(bf16[1536,1536]{1,0:T(8,128)(2,1)S(1)} %get-tuple-element.19.panel, bf16[32,1536]{1,0:T(8,128)(2,1)S(1)} %collective-permute-done.2.other, f32[32,1536]{1,0:T(8,128)S(1)} %half.3.part, f32[32,1536]{1,0:T(8,128)S(1)} %get-tuple-element.23.second, f32[32,32]{1,0:T(8,128)S(1)} %gram.1, ...), custom_call_target="tpu_custom_call" | custom-call | tf_op jit(solution)/shard_map/image/pallas_call | solution.py:311
  32.6 0.3 collective-permute-start.4
  32.9 0.8 %ritz.1 = f32[32,192]{1,0:T(8,128)} custom-call(f32[32,32]{1,0:T(8,128)S(1)} %get-tuple-element.24.inverse, f32[32,1536]{1,0:T(8,128)S(1)} %get-tuple-element.23.second), custom_call_target="tpu_custom_call" | custom-call | tf_op jit(solution)/shard_map/ritz/pallas_call | solution.py:318
  33.7 0.1 collective-permute-done.4.cross_other
  33.8 0.9 %projected.1 = f32[32,32]{1,0:T(8,128)} custom-call(f32[32,32]{1,0:T(8,128)S(1)} %get-tuple-element.24.inverse, f32[32,32]{1,0:T(8,128)S(1)} %get-tuple-element.25.cross, f32[32,32]{1,0:T(8,128)S(1)} %collective-permute-done.4.cross_other), custom_call_target="tpu_custom_call" | custom-call | tf_op jit(solution)/shard_map/projected/pallas_call | solution.py:321
Async XLA Ops:
  16.5 5.1 %collective-permute-start = (bf16[8,48,256]{2,1,0:T(8,128)(2,1)S(1)}, bf16[8,48,256]{2,1,0:T(8,128)(2,1)S(1)}, u32[]{:S(2)}, u32[]{:S(2)}) collective-permute-start(bf16[8,48,256]{2,1,0:T(8,128)(2,1)S(1)} %all_to_all.5.own), channel_id=1, source_target_pairs={{0,1},{1,0},{2,3},{3,2},{4,5},{5,4},{6,7},{7,6},{8,9},{9,8},{10,11... | collective-permute-start | bytes 589832 | tf_op jit(solution)/shard_map/ppermute | solution.py:279
  25.5 1.5 %collective-permute-start.1 = (bf16[32,1536]{1,0:T(8,128)(2,1)S(1)}, bf16[32,1536]{1,0:T(8,128)(2,1)S(1)}, u32[]{:S(2)}, u32[]{:S(2)}) collective-permute-start(bf16[32,1536]{1,0:T(8,128)(2,1)S(1)} %get-tuple-element.20.own), channel_id=1, source_target_pairs={{0,1},{1,0},{2,3},{3,2},{4,5},{5,4},{6,7},{7,6},{8,9},{9,8},{10,11... | collective-permute-start | bytes 294920 | tf_op jit(solution)/shard_map/ppermute | solution.py:301
  27.9 1.9 %collective-permute-start.2 = (bf16[32,1536]{1,0:T(8,128)(2,1)S(1)}, bf16[32,1536]{1,0:T(8,128)(2,1)S(1)}, u32[]{:S(2)}, u32[]{:S(2)}) collective-permute-start(bf16[32,1536]{1,0:T(8,128)(2,1)S(1)} %get-tuple-element.22.own), channel_id=1, source_target_pairs={{0,1},{1,0},{2,3},{3,2},{4,5},{5,4},{6,7},{7,6},{8,9},{9,8},{10,11... | collective-permute-start | bytes 294920 | tf_op jit(solution)/shard_map/ppermute | solution.py:308
  28.7 1.2 %collective-permute-start.3 = (f32[32,32]{1,0:T(8,128)S(1)}, f32[32,32]{1,0:T(8,128)S(1)}, u32[]{:S(2)}, u32[]{:S(2)}) collective-permute-start(f32[32,32]{1,0:T(8,128)S(1)} %gram.1), channel_id=1, source_target_pairs={{0,1},{1,0},{2,3},{3,2},{4,5},{5,4},{6,7},{7,6},{8,9},{9,8},{10,11... | collective-permute-start | bytes 12296 | tf_op jit(solution)/shard_map/ppermute | solution.py:310
  32.6 1.2 %collective-permute-start.4 = (f32[32,32]{1,0:T(8,128)S(1)}, f32[32,32]{1,0:T(8,128)S(1)}, u32[]{:S(2)}, u32[]{:S(2)}) collective-permute-start(f32[32,32]{1,0:T(8,128)S(1)} %get-tuple-element.25.cross), channel_id=1, source_target_pairs={{0,1},{1,0},{2,3},{3,2},{4,5},{5,4},{6,7},{7,6},{8,9},{9,8},{10,11... | collective-permute-start | bytes 12296 | tf_op jit(solution)/shard_map/ppermute | solution.py:317

commit v5 on v4

--- a/solution.py
+++ b/solution.py
@@ -17,8 +17,9 @@
 HIGHEST = lax.Precision.HIGHEST
 VMEM_SPEC = pl.BlockSpec(memory_space=pltpu.VMEM)
 WIDTH = 192
-TILE_ROWS = 512
-TILE_COLS = 256
+CHUNK = 256
+TALL = 256
+PIVOTS = 8
 
 
 def pieces(x):
@@ -37,9 +38,14 @@
         copy.wait()
     geometry, nets, layers, modes, _, sheet = scratch
     high, mid, low = pieces(geometry[...])
-    zeros = jnp.zeros((2, WIDTH), F32)
     rows = jnp.concatenate(
-        [high, nets[...].astype(F32), layers[...].astype(F32), mid, zeros, low, zeros], axis=0
+        [
+            *(high[2:5], mid[2:5], high[0:2]),
+            *(high[2:5], low[2:5], mid[0:2]),
+            *(low[0:2], high[5:6], mid[5:6], low[5:6]),
+            *(nets[...].astype(F32), layers[...].astype(F32), jnp.zeros((1, WIDTH), F32)),
+        ],
+        axis=0,
     )
     sheet[...] = jnp.zeros_like(sheet)
     sheet[0:32, 0:WIDTH] = modes[...].astype(F32)
@@ -65,109 +71,133 @@
         stage[40:56, start + 128 : start + 192] = sheet[32:48, 128:192]
 
 
-def net_groups(base, nets):
-    listed = [base] + [jnp.where(nets == float(n), base, 0.0) for n in range(NETS)]
-    return jnp.concatenate(listed, axis=0)
-
-
-def left_operand(stage, left):
+def signs(stage):
+    net = stage[53:54, :]
+    upper = jnp.where(net >= 2.0, 1.0, 0.0)
+    a = 1.0 - 2.0 * (net - 2.0 * upper)
+    b = 1.0 - 2.0 * upper
+    return a, b, a * b
+
+
+def squares(stage):
+    return pieces(jnp.square(stage[50:51, :] + stage[51:52, :] + stage[52:53, :]))
+
+
+def left_operand(stage, left, feats, tall):
     length = stage.shape[1]
-    nets = stage[38:39, :]
-    segment = [net_groups(stage[s + 2 : s + 5, :], nets) for s in (32, 40, 48)]
-    place_x = [stage[s : s + 1, :] for s in (32, 40, 48)]
-    place_y = [stage[s + 1 : s + 2, :] for s in (32, 40, 48)]
-    spare = place_x + place_y
-    for index, piece in enumerate((0, 0, 1, 1, 0, 2)):
-        left[16 * index : 16 * index + 16, :] = jnp.concatenate([segment[piece], spare[index]], axis=0)
+    base = stage[32:40, :]
+    fine = stage[40:48, :]
+    left[0:8, :] = base
+    left[32:40, :] = base
+    left[64:72, :] = fine
+    for index, sign in enumerate(signs(stage)):
+        at = 8 * index + 8
+        signed = base * sign
+        left[at : at + 8, :] = signed
+        left[32 + at : 40 + at, :] = signed
+        left[64 + at : 72 + at, :] = fine * sign
     levels = lax.broadcasted_iota(jnp.int32, (LAYERS, length), 0).astype(F32)
-    chosen = jnp.where(levels == stage[39:40, :], 1.0, 0.0)
+    chosen = jnp.where(levels == stage[54:55, :], 1.0, 0.0)
     left[96:104, :] = chosen
     left[104:112, :] = chosen
     left[112:120, :] = chosen
-    ones = jnp.ones((3, length), F32)
-    left[120:128, :] = jnp.concatenate([*squares(stage), ones, jnp.zeros((2, length), F32)], axis=0)
-
-
-def squares(stage):
-    return pieces(jnp.square(stage[37:38, :] + stage[45:46, :] + stage[53:54, :]))
+    left[120:128, :] = jnp.concatenate([*squares(stage), jnp.ones((3, length), F32), stage[48:50, :]], axis=0)
+    line = lax.broadcasted_iota(jnp.int32, (128, 256), 0)
+    lane = lax.broadcasted_iota(jnp.int32, (128, 256), 1)
+    for_x = (lane < 128) & ((line == 6) | (line == 70) | (line == 126))
+    for_y = (lane >= 128) & ((line == 7) | (line == 71) | (line == 127))
+    columns = jnp.where(for_x | for_y, 1.0, 0.0).astype(BF16)
+    for start in range(0, length, CHUNK):
+        here = slice(start, start + CHUNK)
+        turned = left[:, here].T.astype(BF16)
+        feats[here, :] = turned
+        tall[here, :] = jnp.dot(turned, columns, preferred_element_type=F32)
 
 
 def right_operand(scale, stage, right, coarse, places):
     cols = stage.shape[1]
-    nets = stage[38:39, :]
-    base = (stage[34:37, :] + stage[42:45, :] + stage[50:53, :]) * (SHIELD_FACTOR * scale)
-    scaled = [net_groups(piece, nets) for piece in pieces(base)]
-    blank = jnp.zeros((1, cols), F32)
-    for index, piece in enumerate((0, 1, 0, 1, 2, 0)):
-        right[16 * index : 16 * index + 16, :] = jnp.concatenate([scaled[piece], blank], axis=0).astype(BF16)
+    rest = (1.0 - SHIELD_FACTOR) / NETS
+    segment = stage[32:35, :] + stage[35:38, :] + stage[43:46, :]
+    blank = jnp.zeros((2, cols), F32)
+
+    def blocks(weight):
+        high, mid, low = pieces(segment * weight)
+        return [jnp.concatenate(pair, axis=0) for pair in ((high, mid, blank), (mid, high, blank), (low, high, blank))]
+
+    plain = blocks((SHIELD_FACTOR + rest) * scale)
+    extra = blocks(rest * scale)
+    for index in range(3):
+        signed = [extra[index] * sign for sign in signs(stage)]
+        right[32 * index : 32 * index + 32, :] = jnp.concatenate([plain[index], *signed], axis=0).astype(BF16)
     right[96:128, :] = jnp.zeros((32, cols), BF16)
     coarse[0:96, :] = jnp.zeros((96, cols), BF16)
     levels = lax.broadcasted_iota(jnp.int32, (LAYERS, cols), 0).astype(F32)
-    gap = levels * LAYER_PITCH - stage[39:40, :] * LAYER_PITCH
-    ones = jnp.ones((3, cols), F32)
+    gap = levels * LAYER_PITCH - stage[54:55, :] * LAYER_PITCH
     coarse[96:128, :] = jnp.concatenate(
-        [*pieces(gap * gap), ones, *squares(stage), jnp.zeros((2, cols), F32)], axis=0
+        [*pieces(gap * gap), jnp.ones((3, cols), F32), *squares(stage), blank], axis=0
     ).astype(BF16)
-    places[...] = stage[32:40, :] + stage[40:48, :] + stage[48:56, :]
-
-
-def place_columns():
-    line = lax.broadcasted_iota(jnp.int32, (128, 256), 0)
-    lane = lax.broadcasted_iota(jnp.int32, (128, 256), 1)
-    for_x = (lane < 128) & ((line == 15) | (line == 31) | (line == 47))
-    for_y = (lane >= 128) & ((line == 63) | (line == 79) | (line == 95))
-    return jnp.where(for_x | for_y, 1.0, 0.0).astype(BF16)
-
-
-def generate(left, right, coarse, places, panel, start):
-    here = slice(start, start + TILE_ROWS)
-    feats = left[:, here].T.astype(BF16)
-    tall = jnp.dot(feats, place_columns(), preferred_element_type=F32)
-    tall_x = jnp.concatenate([tall[:, 0:128]] * (TILE_COLS // 128), axis=1)
-    tall_y = jnp.concatenate([tall[:, 128:256]] * (TILE_COLS // 128), axis=1)
-    for first in range(0, panel.shape[1], TILE_COLS):
-        there = slice(first, first + TILE_COLS)
-        aligned = jnp.dot(feats, right[:, there], preferred_element_type=F32)
-        spread = jnp.dot(feats, coarse[:, there], preferred_element_type=F32)
-        delta_x = tall_x - places[0:1, there]
-        delta_y = tall_y - places[1:2, there]
-        spread = delta_x * delta_x + delta_y * delta_y + spread
-        panel[here, there] = (aligned * lax.rsqrt(spread)).astype(BF16)
-
-
-def partial_product(modes, panel, start):
-    here = slice(start, start + TILE_ROWS)
-    return jnp.dot(modes[:, here], panel[here, :], preferred_element_type=F32)
-
-
-def own_tiles_body(scale, own, panel, right, coarse, places, modes, total, stage, left):
+    places[0:2, :] = stage[38:40, :] + stage[46:48, :] + stage[48:50, :]
+    places[2:8, :] = jnp.zeros((6, cols), F32)
+
+
+def generate(feats, tall, right, coarse, places, panel, first, start):
+    for top in range(first, panel.shape[0], TALL):
+        generate_rows(feats, tall, right, coarse, places, panel, slice(top, min(top + TALL, panel.shape[0])), start)
+
+
+def generate_rows(feats, tall, right, coarse, places, panel, here, start):
+    there = slice(start, start + CHUNK)
+    rows = feats[here, :]
+    aligned = jnp.dot(rows, right[:, there], preferred_element_type=F32)
+    spread = jnp.dot(rows, coarse[:, there], preferred_element_type=F32)
+    tall_x = jnp.concatenate([tall[here, 0:128]] * (CHUNK // 128), axis=1)
+    tall_y = jnp.concatenate([tall[here, 128:256]] * (CHUNK // 128), axis=1)
+    delta_x = tall_x - places[0:1, there]
+    delta_y = tall_y - places[1:2, there]
+    spread = delta_x * delta_x + delta_y * delta_y + spread
+    panel[here, there] = (aligned * lax.rsqrt(spread)).astype(BF16)
+
+
+def own_tiles_body(scale, own, panel, right, coarse, places, modes, total, stage, left, feats, tall):
     unpack(own, stage)
-    left_operand(stage, left)
+    left_operand(stage, left, feats, tall)
     right_operand(scale, stage, right, coarse, places)
     modes[...] = stage[0:32, :].astype(BF16)
     cols = panel.shape[0]
-    generate(left, right, coarse, places, panel, 0)
-    for start in range(TILE_ROWS, cols, TILE_ROWS):
-        done = partial_product(modes, panel, start - TILE_ROWS)
-        total[...] = done if start == TILE_ROWS else total[...] + done
-        generate(left, right, coarse, places, panel, start)
-    total[...] += partial_product(modes, panel, cols - TILE_ROWS)
-
-
-def other_tiles_body(other, right, coarse, places, modes, total, low_edge, high_edge, panel, filtered, stage, left, others):
+
+    def multiply(start):
+        there = slice(start, start + CHUNK)
+        total[:, there] = jnp.dot(modes[...], panel[:, there], preferred_element_type=F32)
+
+    for start in range(0, cols, CHUNK):
+        if start > 0:
+            multiply(start - CHUNK)
+        generate(feats, tall, right, coarse, places, panel, start, start)
+        there = slice(start, start + CHUNK)
+        for other in range(0, start, CHUNK):
+            panel[other : other + CHUNK, there] = panel[there, other : other + CHUNK].T
+    multiply(cols - CHUNK)
+
+
+def other_tiles_body(other, right, coarse, places, modes, total, low_edge, high_edge, panel, filtered, *scratch):
+    stage, left, feats, tall, others = scratch
     unpack(other, stage)
-    left_operand(stage, left)
+    left_operand(stage, left, feats, tall)
     others[...] = stage[0:32, :].astype(BF16)
     cols = panel.shape[0]
-    applied = total[...]
-    generate(left, right, coarse, places, panel, 0)
-    for start in range(TILE_ROWS, cols, TILE_ROWS):
-        applied = applied + partial_product(others, panel, start - TILE_ROWS)
-        generate(left, right, coarse, places, panel, start)
-    applied = applied + partial_product(others, panel, cols - TILE_ROWS)
     centre = (low_edge[...] + high_edge[...]) * 0.5
     half_width = (high_edge[...] - low_edge[...]) * 0.5
-    filtered[...] = ((applied - centre * modes[...].astype(F32)) / half_width).astype(BF16)
+
+    def multiply(start):
+        there = slice(start, start + CHUNK)
+        applied = total[:, there] + jnp.dot(others[...], panel[:, there], preferred_element_type=F32)
+        filtered[:, there] = ((applied - centre * modes[:, there].astype(F32)) / half_width).astype(BF16)
+
+    for start in range(0, cols, CHUNK):
+        if start > 0:
+            multiply(start - CHUNK)
+        generate(feats, tall, right, coarse, places, panel, 0, start)
+    multiply(cols - CHUNK)
 
 
 def half_body(panel, own, part):
@@ -191,19 +221,32 @@
     gram[...] = outer(second[...], second[...]) / filaments
 
 
+def eliminate(system, modes):
+    line = lax.broadcasted_iota(jnp.int32, system.shape, 0)
+    for first in range(0, modes, PIVOTS):
+        step = range(first, first + PIVOTS)
+        columns = {k: jnp.broadcast_to(system[:, k : k + 1], system.shape) for k in step}
+        rows = {k: system[k : k + 1, :] for k in step}
+        weights = {}
+        for k in step:
+            weights[k] = jnp.where(line > k, columns[k] / columns[k][k : k + 1, :], 0.0)
+            for later in range(k + 1, first + PIVOTS):
+                columns[later] = columns[later] - weights[k] * columns[k][later : later + 1, :]
+                rows[later] = rows[later] - weights[k][later : later + 1, :] * rows[k]
+        for k in step:
+            system = system - weights[k] * rows[k]
+    return system
+
+
 def image_body(filaments, panel, other, part, second, gram, gram_other, cross, inverse):
     modes = gram.shape[0]
     line = lax.broadcasted_iota(jnp.int32, (modes, modes), 0)
     lane = lax.broadcasted_iota(jnp.int32, (modes, modes), 1)
     unit = jnp.where(lane == line, 1.0, 0.0)
-    system = jnp.concatenate([gram[...] + gram_other[...], unit], axis=1)
+    system = jnp.concatenate([gram[...] + gram_other[...], unit, unit, unit], axis=1)
     applied = part[...] + jnp.dot(other[...], panel[...], preferred_element_type=F32)
     cross[...] = outer(second[...], applied) / filaments
-    for pivot in range(modes):
-        row = system[pivot : pivot + 1, :]
-        column = system[:, pivot : pivot + 1] / system[pivot : pivot + 1, pivot : pivot + 1]
-        column = jnp.where(line[:, 0:1] > pivot, column, 0.0)
-        system = system - column * row
+    system = eliminate(system, modes)
     diagonal = jnp.sum(system[:, 0:modes] * unit, axis=1, keepdims=True)
     inverse[...] = system[:, modes : 2 * modes] / jnp.sqrt(diagonal)
 
@@ -279,7 +322,12 @@
     other = lax.ppermute(own, "col", pair)
     square = pltpu.VMEM((cols, cols), BF16)
     operand = shape((128, cols), BF16)
-    stages = [pltpu.VMEM((64, cols), F32), pltpu.VMEM((128, cols), F32)]
+    stages = [
+        pltpu.VMEM((56, cols), F32),
+        pltpu.VMEM((128, cols), F32),
+        pltpu.VMEM((cols, 128), BF16),
+        pltpu.VMEM((cols, 256), F32),
+    ]
     panel_own, right, coarse, places, low, total = call(
         functools.partial(own_tiles_body, 1.0 / math.sqrt(rows)),
         "own_tiles",
@@ -412,8 +460,7 @@
         and (count // 2) % 2 == 0
         and modes == 32
         and width == WIDTH
-        and (rows // 2) % TILE_COLS == 0
-        and (rows // 2) % TILE_ROWS == 0
+        and (rows // 2) % CHUNK == 0
         and rows * rows <= 16 * 1024 * 1024
     )
 

time: 35.1 us -> 32.6 us (0.929)
  Pallas kernels: 16.1 us -> 13.6 us
    pallas_call x1, Pallas kernels: 2.78 us -> 1.22 us  [paired_shards(): call(functools.partial(image_body, float(rows)), 'image', (shape((modes,...]
    pallas_call x1, Pallas kernels: 3.84 us -> 2.83 us  [paired_shards(): call(functools.partial(own_tiles_body, 1.0 / math.sqrt(rows)), 'own_tiles...]
  transfers between devices with their start and end apart: 5 -> 5, of which waited for: 2 -> 2; matrix products, arithmetic and copies ran while one was open for 0% -> 0% of each run, Pallas kernels for 20% -> 18%
where the time goes in v5:
time: 32.6 us; the launch traced here: 32.3 us
  blocking collectives  15 us (46%)
  Pallas kernels  13.6 us (42%)
  between operations  1.96 us (6%)
  starting transfers between devices  1.43 us (4%)
    all_to_all x1, blocking collectives, paired_shards(): lax.all_to_all(packed, ('fil', 'col'), 0, 0, axis_index_groups=same_core,...  15 us
    pallas_call x1, Pallas kernels, paired_shards(): call(other_tiles_body, 'other_tiles', (square, shape((modes, cols), BF16)...  3.88 us
    pallas_call x1, Pallas kernels, paired_shards(): call(functools.partial(own_tiles_body, 1.0 / math.sqrt(rows)), 'own_tiles...  2.83 us
    pallas_call x1, Pallas kernels, paired_shards(): call(functools.partial(image_body, float(rows)), 'image', (shape((modes,...  1.22 us
    pallas_call x1, Pallas kernels, paired_shards(): call(second_body, 'second', (shape((modes, cols), F32), shape((modes, col...  0.92 us
    pallas_call x1, Pallas kernels, paired_shards(): call(projected_body, 'projected', shape((modes, modes), F32), [VMEM_SPEC]...  0.91 us
    pallas_call x1, Pallas kernels, paired_shards(): call(pack_body, 'pack', shape((count, 48, 256), BF16), [pl.BlockSpec(memo...  0.9 us
    pallas_call x1, Pallas kernels, paired_shards(): half(panel_own, filtered)  0.9 us
  transfers between devices with their start and end apart: 5, of which 2 were waited for; matrix products, arithmetic and copies ran while one was open for 0% of the time, Pallas kernels for 18%

profile of v5, /device:TPU:0, one launch (start us, length us, event | category | flops | bytes accessed | tf_op | source)
XLA Modules:
  0.0 32.3 jit_solution(9552323690668186334)
XLA Ops:
  0.6 0.9 %pack.1 = bf16[8,48,256]{2,1,0:T(8,128)(2,1)S(1)} custom-call(f32[6,192]{1,0:T(8,128)} %geometry.1, s32[1,192]{1,0:T(1,128)} %bitcast.12, s32[1,192]{1,0:T(1,128)} %bitcast.13, bf16[32,192]{1,0:T(8,128)(2,1)} %bitcast.11), custom_call_target="tpu_custom_call" | custom-call | tf_op jit(solution)/shard_map/pack/pallas_call | solution.py:296
  1.5 15.0 %all_to_all.5.own = bf16[8,48,256]{2,1,0:T(8,128)(2,1)S(1)} all-to-all(bf16[8,48,256]{2,1,0:T(8,128)(2,1)S(1)} %pack.1), channel_id=1, replica_groups={{0,2,4,6,8,10,12,14},{1,3,5,7,9,11,13,15},{16,18,20,22,24,26,28,30},{17..., dimensions={0} | all-to-all | bytes 393216 | tf_op jit(solution)/shard_map/all_to_all | solution.py:321
  16.5 0.0 collective-permute-start
  17.8 2.8 %own_tiles.1 = (bf16[1536,1536]{1,0:T(8,128)(2,1)S(1)}, bf16[128,1536]{1,0:T(8,128)(2,1)S(1)}, bf16[128,1536]{1,0:T(8,128)(2,1)S(1)}, f32[8,1536]{1,0:T(8,128)S(...) custom-call(bf16[8,48,256]{2,1,0:T(8,128)(2,1)S(1)} %all_to_all.5.own), custom_call_target="tpu_custom_call" | custom-call | flops 754974720 | tf_op jit(solution)/shard_map/own_tiles/pallas_call | solution.py:331
  20.7 0.0 collective-permute-done.other
  20.7 3.9 %other_tiles.1 = (bf16[1536,1536]{1,0:T(8,128)(2,1)S(1)}, bf16[32,1536]{1,0:T(8,128)(2,1)S(1)}) custom-call(bf16[8,48,256]{2,1,0:T(8,128)(2,1)S(1)} %collective-permute-done.other, bf16[128,1536]{1,0:T(8,128)(2,1)S(1)} %get-tuple-element.14.right, bf16[128,1536]{1,0:T(8,128)(2,1)S(1)} %get-tuple-element.15.coarse, f32[8,1536]{1,0:T(8,128)S(1)} %get-tuple-element.16.places, ...), custom_call_target="tpu_custom_call" | custom-call | flops 754974720 | tf_op jit(solution)/shard_map/other_tiles/pallas_call | solution.py:339
  24.6 0.6 %collective-permute-start.1 = (bf16[32,1536]{1,0:T(8,128)(2,1)S(1)}, bf16[32,1536]{1,0:T(8,128)(2,1)S(1)}, u32[]{:S(2)}, u32[]{:S(2)}) collective-permute-start(bf16[32,1536]{1,0:T(8,128)(2,1)S(1)} %get-tuple-element.20.own), channel_id=1, source_target_pairs={{0,1},{1,0},{2,3},{3,2},{4,5},{5,4},{6,7},{7,6},{8,9},{9,8},{10,11... | collective-permute-start | bytes 294920 | tf_op jit(solution)/shard_map/ppermute | solution.py:349
  25.1 0.9 %half.2.part = f32[32,1536]{1,0:T(8,128)S(1)} custom-call(bf16[1536,1536]{1,0:T(8,128)(2,1)S(1)} %get-tuple-element.21.panel, bf16[32,1536]{1,0:T(8,128)(2,1)S(1)} %get-tuple-element.20.own), custom_call_target="tpu_custom_call" | custom-call | flops 150994944 | tf_op jit(solution)/shard_map/half/pallas_call | solution.py:355
  26.0 0.0 collective-permute-done.1.other
  26.1 0.9 %second.1 = (f32[32,1536]{1,0:T(8,128)S(1)}, bf16[32,1536]{1,0:T(8,128)(2,1)S(1)}) custom-call(bf16[1536,1536]{1,0:T(8,128)(2,1)S(1)} %get-tuple-element.19.panel, bf16[32,1536]{1,0:T(8,128)(2,1)S(1)} %collective-permute-done.1.other, f32[32,1536]{1,0:T(8,128)S(1)} %half.2.part, bf16[32,1536]{1,0:T(8,128)(2,1)S(1)} %get-tuple-element.20.own, ...), custom_call_target="tpu_custom_call" | custom-call | tf_op jit(solution)/shard_map/second/pallas_call | solution.py:350
  27.0 0.4 %collective-permute-start.2 = (bf16[32,1536]{1,0:T(8,128)(2,1)S(1)}, bf16[32,1536]{1,0:T(8,128)(2,1)S(1)}, u32[]{:S(2)}, u32[]{:S(2)}) collective-permute-start(bf16[32,1536]{1,0:T(8,128)(2,1)S(1)} %get-tuple-element.22.own), channel_id=1, source_target_pairs={{0,1},{1,0},{2,3},{3,2},{4,5},{5,4},{6,7},{7,6},{8,9},{9,8},{10,11... | collective-permute-start | bytes 294920 | tf_op jit(solution)/shard_map/ppermute | solution.py:356
  27.4 0.3 gram.1
  27.7 0.2 collective-permute-start.3
  27.9 0.9 %half.3.part = f32[32,1536]{1,0:T(8,128)S(1)} custom-call(bf16[1536,1536]{1,0:T(8,128)(2,1)S(1)} %get-tuple-element.21.panel, bf16[32,1536]{1,0:T(8,128)(2,1)S(1)} %get-tuple-element.22.own), custom_call_target="tpu_custom_call" | custom-call | flops 150994944 | tf_op jit(solution)/shard_map/half/pallas_call | solution.py:364
  28.8 0.1 collective-permute-done.3.gram_other
  28.9 0.0 collective-permute-done.2.other
  28.9 1.2 %image.1 = (f32[32,32]{1,0:T(8,128)S(1)}, f32[32,32]{1,0:T(8,128)S(1)}) custom-call(bf16[1536,1536]{1,0:T(8,128)(2,1)S(1)} %get-tuple-element.19.panel, bf16[32,1536]{1,0:T(8,128)(2,1)S(1)} %collective-permute-done.2.other, f32[32,1536]{1,0:T(8,128)S(1)} %half.3.part, f32[32,1536]{1,0:T(8,128)S(1)} %get-tuple-element.23.second, f32[32,32]{1,0:T(8,128)S(1)} %gram.1, ...), custom_call_target="tpu_custom_call" | custom-call | tf_op jit(solution)/shard_map/image/pallas_call | solution.py:359
  30.1 0.3 collective-permute-start.4
  30.4 0.8 %ritz.1 = f32[32,192]{1,0:T(8,128)} custom-call(f32[32,32]{1,0:T(8,128)S(1)} %get-tuple-element.24.inverse, f32[32,1536]{1,0:T(8,128)S(1)} %get-tuple-element.23.second), custom_call_target="tpu_custom_call" | custom-call | tf_op jit(solution)/shard_map/ritz/pallas_call | solution.py:366
  31.3 0.1 collective-permute-done.4.cross_other
  31.3 0.9 %projected.1 = f32[32,32]{1,0:T(8,128)} custom-call(f32[32,32]{1,0:T(8,128)S(1)} %get-tuple-element.24.inverse, f32[32,32]{1,0:T(8,128)S(1)} %get-tuple-element.25.cross, f32[32,32]{1,0:T(8,128)S(1)} %collective-permute-done.4.cross_other), custom_call_target="tpu_custom_call" | custom-call | tf_op jit(solution)/shard_map/projected/pallas_call | solution.py:369
Async XLA Ops:
  16.5 4.1 %collective-permute-start = (bf16[8,48,256]{2,1,0:T(8,128)(2,1)S(1)}, bf16[8,48,256]{2,1,0:T(8,128)(2,1)S(1)}, u32[]{:S(2)}, u32[]{:S(2)}) collective-permute-start(bf16[8,48,256]{2,1,0:T(8,128)(2,1)S(1)} %all_to_all.5.own), channel_id=1, source_target_pairs={{0,1},{1,0},{2,3},{3,2},{4,5},{5,4},{6,7},{7,6},{8,9},{9,8},{10,11... | collective-permute-start | bytes 589832 | tf_op jit(solution)/shard_map/ppermute | solution.py:322
  24.6 1.5 %collective-permute-start.1 = (bf16[32,1536]{1,0:T(8,128)(2,1)S(1)}, bf16[32,1536]{1,0:T(8,128)(2,1)S(1)}, u32[]{:S(2)}, u32[]{:S(2)}) collective-permute-start(bf16[32,1536]{1,0:T(8,128)(2,1)S(1)} %get-tuple-element.20.own), channel_id=1, source_target_pairs={{0,1},{1,0},{2,3},{3,2},{4,5},{5,4},{6,7},{7,6},{8,9},{9,8},{10,11... | collective-permute-start | bytes 294920 | tf_op jit(solution)/shard_map/ppermute | solution.py:349
  27.0 1.9 %collective-permute-start.2 = (bf16[32,1536]{1,0:T(8,128)(2,1)S(1)}, bf16[32,1536]{1,0:T(8,128)(2,1)S(1)}, u32[]{:S(2)}, u32[]{:S(2)}) collective-permute-start(bf16[32,1536]{1,0:T(8,128)(2,1)S(1)} %get-tuple-element.22.own), channel_id=1, source_target_pairs={{0,1},{1,0},{2,3},{3,2},{4,5},{5,4},{6,7},{7,6},{8,9},{9,8},{10,11... | collective-permute-start | bytes 294920 | tf_op jit(solution)/shard_map/ppermute | solution.py:356
  27.7 1.2 %collective-permute-start.3 = (f32[32,32]{1,0:T(8,128)S(1)}, f32[32,32]{1,0:T(8,128)S(1)}, u32[]{:S(2)}, u32[]{:S(2)}) collective-permute-start(f32[32,32]{1,0:T(8,128)S(1)} %gram.1), channel_id=1, source_target_pairs={{0,1},{1,0},{2,3},{3,2},{4,5},{5,4},{6,7},{7,6},{8,9},{9,8},{10,11... | collective-permute-start | bytes 12296 | tf_op jit(solution)/shard_map/ppermute | solution.py:358
  30.1 1.2 %collective-permute-start.4 = (f32[32,32]{1,0:T(8,128)S(1)}, f32[32,32]{1,0:T(8,128)S(1)}, u32[]{:S(2)}, u32[]{:S(2)}) collective-permute-start(f32[32,32]{1,0:T(8,128)S(1)} %get-tuple-element.25.cross), channel_id=1, source_target_pairs={{0,1},{1,0},{2,3},{3,2},{4,5},{5,4},{6,7},{7,6},{8,9},{9,8},{10,11... | collective-permute-start | bytes 12296 | tf_op jit(solution)/shard_map/ppermute | solution.py:365
